TPU v7x, 128 devices: a whole 4x4x4 slice. The times are simulated.
128 devices in a mesh: pop: 8 (over z, y_lo), mp: 16 (over x, y_hi, core).
Axes of the slice: x: 4, y: 4 (y_hi: 2, y_lo: 2; y = y_hi * 2 + y_lo), z: 4, core: 2. Of those that a mesh axis runs over, the one named last changes fastest.
Arguments:
- tokens: bfloat16 [4096, 3584], P('pop', 'mp'), may hold values from -6 to 6
- w_gate: bfloat16 [3584, 18944], P(None, 'mp'), may hold values from -0.09375 to 0.09375
- w_up: bfloat16 [3584, 18944], P(None, 'mp'), may hold values from -0.09375 to 0.09375
- a_gate: bfloat16 [2048, 4, 3584], P('pop', None, 'mp'), may hold values from -0.125 to 0.125
- a_up: bfloat16 [2048, 4, 3584], P('pop', None, 'mp'), may hold values from -0.09375 to 0.09375
- b_gate: bfloat16 [2048, 4, 18944], P('pop', None, 'mp'), may hold values from -6 to 6
- b_up: bfloat16 [2048, 4, 18944], P('pop', None, 'mp'), may hold values from -6 to 6
- fitness: float32 [2048], P('pop'), may hold values from -4 to 4
Outputs:
- hidden: bfloat16 [4096, 18944], P('pop', 'mp')
- new_gate: bfloat16 [3584, 18944], P('pop', 'mp')
- new_up: bfloat16 [3584, 18944], P('pop', 'mp')
All inputs are finite; a program needn't handle non-finite values.
Results may differ from a plain program's by a relative error of at most 0.015.
Values may be sent and summed in bfloat16 or wider, within the bound.
No kernel may reach another device: no remote copies, remote signals or barrier semaphores. Data moves between devices by JAX's collectives and lax.ppermute only.
A program may use at most 192 MiB of HBM per device.

v0:
```python
import jax
import jax.numpy as jnp
from jax import lax
from jax.sharding import PartitionSpec as P

noise_scale = 0.5


def perturbed(gathered, weight, probe_vector, second_factor):
    base_part = jnp.dot(gathered, weight, preferred_element_type=jnp.float32)
    lowrank_noise = jnp.einsum(
        "axg,agq->axq",
        probe_vector.astype(jnp.bfloat16),
        second_factor,
        preferred_element_type=jnp.float32,
    )
    return base_part + noise_scale * lowrank_noise.reshape(base_part.shape)


def update_maker(full_fac, second_factor, step_coeff, row_span):
    group_rows = full_fac.shape[0] * full_fac.shape[1]
    right_side = second_factor.reshape(group_rows, second_factor.shape[2])
    left_side = full_fac.reshape(group_rows, row_span)
    product = lax.dot_general(
        left_side, right_side, (((0,), (0,)), ((), ())), preferred_element_type=jnp.float32
    )
    return step_coeff * product


def local(tokens, w_gate, w_up, a_gate, a_up, b_gate, b_up, fitness):
    member_count = a_gate.shape[0]
    rank_count = a_gate.shape[1]
    gathered = lax.all_gather(tokens, "mp", axis=1, tiled=True)
    fit_column = fitness[:, None, None]
    own_part = tokens.reshape(member_count, 2, tokens.shape[1])
    part_gate = jnp.einsum("mtd,mrd->mtr", own_part, a_gate, preferred_element_type=jnp.float32)
    part_upper = jnp.einsum("mtd,mrd->mtr", own_part, a_up, preferred_element_type=jnp.float32)
    probe_g, probe_u = lax.psum((part_gate, part_upper), "mp")
    gate_pre = perturbed(gathered, w_gate, probe_g, b_gate)
    up_pre = perturbed(gathered, w_up, probe_u, b_up)
    hidden = (jax.nn.silu(gate_pre) * up_pre).astype(jnp.bfloat16)
    weighted_gate = (fit_column * a_gate.astype(jnp.float32)).astype(jnp.bfloat16)
    scaled_u = (fit_column * a_up.astype(jnp.float32)).astype(jnp.bfloat16)
    full_g, full_u = (
        lax.all_gather(weighted_gate, "mp", axis=2, tiled=True),
        lax.all_gather(scaled_u, "mp", axis=2, tiled=True),
    )
    pop_size = lax.axis_size("pop")
    step_coeff = 1.0 / jnp.sqrt(jnp.float32(member_count * pop_size * rank_count))
    row_count = w_gate.shape[0] // pop_size
    first_own = lax.axis_index("pop") * row_count
    total_g = lax.psum_scatter(
        update_maker(full_g, b_gate, step_coeff, row_count * lax.axis_size("pop")).astype(
            jnp.bfloat16
        ),
        "pop",
        scatter_dimension=0,
        tiled=True,
    ).astype(jnp.float32)
    total_u = lax.psum_scatter(
        update_maker(full_u, b_up, step_coeff, row_count * lax.axis_size("pop")).astype(
            jnp.bfloat16
        ),
        "pop",
        scatter_dimension=0,
        tiled=True,
    ).astype(jnp.float32)
    local_gate = lax.dynamic_slice_in_dim(w_gate, first_own, row_count, 0)
    own_upper = lax.dynamic_slice_in_dim(w_up, first_own, row_count, 0)
    new_gate = (local_gate.astype(jnp.float32) + total_g).astype(jnp.bfloat16)
    new_up = (own_upper.astype(jnp.float32) + total_u).astype(jnp.bfloat16)
    return (hidden, new_gate, new_up)


def solution(mesh):
    placed = (
        P("pop", "mp"),
        P(None, "mp"),
        P(None, "mp"),
        P("pop", None, "mp"),
        P("pop", None, "mp"),
        P("pop", None, "mp"),
        P("pop", None, "mp"),
        P("pop"),
    )
    return jax.shard_map(
        local,
        mesh=mesh,
        in_specs=placed,
        out_specs=(P("pop", "mp"), P("pop", "mp"), P("pop", "mp")),
        check_vma=False,
    )
```

profile of v0, /device:TPU:1, one launch (start us, length us, event | category | flops | bytes accessed | tf_op | source)
XLA Modules:
  0.0 594.2 jit_solution(13094001607388805031)
XLA Ops:
  7.2 0.0 copy-start.1
  7.2 0.0 all-gather.6.cloned.1.call-start
  7.2 2.4 multiply_convert_fusion
  9.6 0.0 all-gather.6.cloned.1.call-update
  9.7 0.0 all-gather.8.cloned.1.call-start
  9.7 0.7 all-gather.8.cloned.1.call-update
  10.4 0.0 all-gather.4.cloned.1.call-start
  10.5 0.7 all-gather.4.cloned.1.call-update
  11.1 0.0 reduce-scatter.3.cloned.1.call-start
  11.2 72.1 %all-gather.6.cloned.1.call-done = bf16[256,4,3584]{0,2,1:T(8,128)(2,1)} async-done(((bf16[256,4,224]{0,2,1:T(8,128)(2,1)}), bf16[256,4,3584]{0,2,1:T(8,128)(2,1)}) %all-gather.6.cloned.1.call-update) | async-done | bytes 7340048 | tf_op jit(solution)/shard_map/all_gather | solution.py:45
  83.3 0.0 copy-done.1
  83.3 15.1 %fusion.1 = bf16[3584,1184]{1,0:T(8,128)(2,1)} fusion(bf16[256,4,3584]{0,2,1:T(8,128)(2,1)} %all-gather.6.cloned.1.call-done, bf16[256,4,1184]{0,2,1:T(8,128)(2,1)S(1)} %copy-done.1), kind=kOutput, calls=%fused_computation.3 | convolution fusion | flops 8699084800 | bytes 18251776 | tf_op jit(solution)/shard_map/dot_general | solution.py:24
  98.3 0.0 copy-start
  98.3 0.0 reduce-scatter.3.cloned.1.call-update
  98.4 0.0 reduce-scatter.5.cloned.1.call-start
  98.4 54.4 %all-gather.8.cloned.1.call-done = bf16[256,4,3584]{0,2,1:T(8,128)(2,1)} async-done(((bf16[256,4,224]{0,2,1:T(8,128)(2,1)}), bf16[256,4,3584]{0,2,1:T(8,128)(2,1)}) %all-gather.8.cloned.1.call-update) | async-done | bytes 7340048 | tf_op jit(solution)/shard_map/all_gather | solution.py:46
  152.8 0.0 copy-done
  152.8 15.1 %fusion = bf16[3584,1184]{1,0:T(8,128)(2,1)} fusion(bf16[256,4,3584]{0,2,1:T(8,128)(2,1)} %all-gather.8.cloned.1.call-done, bf16[256,4,1184]{0,2,1:T(8,128)(2,1)S(1)} %copy-done), kind=kOutput, calls=%fused_computation.1 | convolution fusion | flops 8699084800 | bytes 18251776 | tf_op jit(solution)/shard_map/dot_general | solution.py:24
  167.9 0.0 reduce-scatter.5.cloned.1.call-update
  167.9 0.0 copy-start.3
  167.9 0.0 copy-start.4
  167.9 4.3 copy.20
  172.2 1.8 copy.17
  173.9 0.0 copy-done.3
  173.9 1.1 copy.25
  175.0 0.0 copy-done.4
  175.0 1.1 copy.24
  176.1 0.0 copy-start.5
  176.1 0.0 copy-start.6
  176.1 5.3 copy.18
  181.4 0.0 copy-done.5
  181.4 0.8 reshape.20
  182.2 1.5 fusion.7
  183.8 0.0 copy-done.6
  183.8 2.1 fusion.6
  185.9 69.8 %all-reduce = (bf16[256,2,4]{2,1,0:T(2,128)(2,1)S(1)}, bf16[256,2,4]{2,1,0:T(2,128)(2,1)S(1)}) all-reduce(f32[256,2,4]{2,1,0:T(2,128)S(1)} %fusion.7, f32[256,2,4]{2,1,0:T(2,128)} %fusion.6), channel_id=1, replica_groups=mesh['pop'=8,'mp'=16] {'mp'}, use_global_device_ids=true, to_apply=%region_1.0 | all-reduce | flops 4096 | bytes 24576 | tf_op jit(solution)/shard_map/psum | solution.py:38
  255.7 3.0 convolution_multiply_fusion
  258.7 3.4 mul.46
  262.1 2.1 copy.21
  264.2 4.8 convolution_multiply_fusion.1
  268.9 3.4 mul.43
  272.3 2.0 copy.19
  274.3 2.0 constant_dynamic-slice_fusion.1
  276.3 0.8 copy.26
  277.1 2.0 constant_dynamic-slice_fusion
  279.1 1.1 copy.27
  280.2 0.0 all-gather.4.cloned.1.call-done
  280.2 0.0 copy-start.2
  280.2 0.0 copy-start.7
  280.2 10.0 %convolution_add_fusion.1 = f32[512,1184]{0,1:T(8,128)S(1)} fusion(f32[512,1184]{0,1:T(8,128)} %copy.19, bf16[3584,1184]{0,1:T(8,128)(2,1)} %param.9, bf16[512,3584]{0,1:T(8,128)(2,1)} %all-gather.4.cloned.1.call-done), kind=kOutput, calls=%fused_computation.8 | convolution fusion | flops 4345905152 | bytes 17006592 | tf_op jit(solution)/shard_map/dot_general | solution.py:10
  290.3 0.0 copy-done.2
  290.3 0.0 copy-done.7
  290.3 9.6 %fusion.3 = bf16[512,1184]{0,1:T(8,128)(2,1)} fusion(f32[512,1184]{0,1:T(8,128)S(1)} %copy-done.2, bf16[3584,1184]{0,1:T(8,128)(2,1)} %param.10, bf16[512,3584]{0,1:T(8,128)(2,1)S(1)} %copy-done.7, f32[512,1184]{0,1:T(8,128)S(1)} %convolution_add_fusion.1), kind=kOutput, calls=%fused_computation.9 | convolution fusion | flops 4349542400 | bytes 18219008 | tf_op jit(solution)/shard_map/dot_general | solution.py:10
  299.9 98.7 %reduce-scatter.3.cloned.1.call-done = bf16[448,1184]{1,0:T(8,128)(2,1)} async-done(((bf16[3584,1184]{1,0:T(8,128)(2,1)}), bf16[448,1184]{1,0:T(8,128)(2,1)}) %reduce-scatter.3.cloned.1.call-update) | async-done | bytes 1060880 | tf_op jit(solution)/shard_map/reduce_scatter | solution.py:52
  398.6 2.5 add_convert_fusion.1
  401.1 184.1 %reduce-scatter.5.cloned.1.call-done = bf16[448,1184]{1,0:T(8,128)(2,1)} async-done(((bf16[3584,1184]{1,0:T(8,128)(2,1)}), bf16[448,1184]{1,0:T(8,128)(2,1)}) %reduce-scatter.5.cloned.1.call-update) | async-done | bytes 1060880 | tf_op jit(solution)/shard_map/reduce_scatter | solution.py:60
  585.2 2.5 add_convert_fusion
Async XLA Ops:
  7.2 76.1 %copy-start.1 = (bf16[256,4,1184]{0,2,1:T(8,128)(2,1)S(1)}, bf16[256,4,1184]{0,2,1:T(8,128)(2,1)}, u32[]{:S(2)}) copy-start(bf16[256,4,1184]{0,2,1:T(8,128)(2,1)} %param.13) | copy-start | bytes 7274500
  7.2 76.1 %all-gather.6.cloned.1.call-start = ((), (), s32[]{:S(2)}) async-start(), calls=%async_computation.3 | async-start | bytes 7798784 | tf_op jit(solution)/shard_map/all_gather | solution.py:45
  9.7 143.1 %all-gather.8.cloned.1.call-start = ((), (), s32[]{:S(2)}) async-start(), calls=%async_computation.5 | async-start | bytes 7798784 | tf_op jit(solution)/shard_map/all_gather | solution.py:46
  10.4 269.8 %all-gather.4.cloned.1.call-start = ((), (), s32[]{:S(2)}) async-start(), calls=%async_computation.2 | async-start | bytes 3899392 | tf_op jit(solution)/shard_map/all_gather | solution.py:33
  11.1 387.4 %reduce-scatter.3.cloned.1.call-start = ((), (), s32[]{:S(2)}) async-start(), calls=%async_computation.4 | async-start | bytes 10321920 | tf_op jit(solution)/shard_map/reduce_scatter | solution.py:52
  98.3 54.4 %copy-start = (bf16[256,4,1184]{0,2,1:T(8,128)(2,1)S(1)}, bf16[256,4,1184]{0,2,1:T(8,128)(2,1)}, u32[]{:S(2)}) copy-start(bf16[256,4,1184]{0,2,1:T(8,128)(2,1)} %param.14) | copy-start | bytes 7274500
  98.4 486.8 %reduce-scatter.5.cloned.1.call-start = ((), (), s32[]{:S(2)}) async-start(), calls=%async_computation.6 | async-start | bytes 10321920 | tf_op jit(solution)/shard_map/reduce_scatter | solution.py:60
  167.9 6.1 %copy-start.3 = (bf16[256,4,224]{0,2,1:T(8,128)(2,1)S(1)}, bf16[256,4,224]{0,2,1:T(8,128)(2,1)}, u32[]{:S(2)}) copy-start(bf16[256,4,224]{0,2,1:T(8,128)(2,1)} %param.12) | copy-start | bytes 1376260
  167.9 7.1 %copy-start.4 = (bf16[256,4,224]{0,2,1:T(8,128)(2,1)S(1)}, bf16[256,4,224]{0,2,1:T(8,128)(2,1)}, u32[]{:S(2)}) copy-start(bf16[256,4,224]{0,2,1:T(8,128)(2,1)} %param.11) | copy-start | bytes 1376260
  176.1 5.4 copy-start.5
  176.1 7.7 %copy-start.6 = (bf16[256,4,224]{2,1,0:T(4,128)(2,1)S(1)}, bf16[256,4,224]{2,1,0:T(4,128)(2,1)}, u32[]{:S(2)}) copy-start(bf16[256,4,224]{2,1,0:T(4,128)(2,1)} %copy.24) | copy-start | bytes 1376260
  280.2 10.1 %copy-start.2 = (f32[512,1184]{0,1:T(8,128)S(1)}, f32[512,1184]{0,1:T(8,128)}, u32[]{:S(2)}) copy-start(f32[512,1184]{0,1:T(8,128)} %copy.21) | copy-start | bytes 7274500
  280.2 10.1 %copy-start.7 = (bf16[512,3584]{0,1:T(8,128)(2,1)S(1)}, bf16[512,3584]{0,1:T(8,128)(2,1)}, u32[]{:S(2)}) copy-start(bf16[512,3584]{0,1:T(8,128)(2,1)} %all-gather.4.cloned.1.call-done) | copy-start | bytes 11010052
Sparse Core Ops, SparseCore 0:
  11.1 72.1 all-gather.5
  86.3 66.4 all-gather.7
  155.2 53.4 all-gather.3
  210.9 187.5 reduce-scatter.2
  400.9 184.2 reduce-scatter.4
where the time goes:
time: 595 us; the launch traced here: 594 us
  waiting for transfers between devices  411 us (69%)
  blocking collectives  69.8 us (12%)
  matrix products  61.2 us (10%)
  local copies, waits for them, and re-layouts  31 us (5%)
  between operations  13.9 us (2%)
  other arithmetic  7.45 us (1%)
    reduce_scatter x1, waiting for transfers between devices, local(): lax.psum_scatter(update_maker(full_u, b_up, step_coeff, row_count * lax.a...  184 us
    reduce_scatter x1, waiting for transfers between devices, local(): lax.psum_scatter(update_maker(full_g, b_gate, step_coeff, row_count * lax...  98.7 us
    all_gather x1, waiting for transfers between devices, local(): lax.all_gather(weighted_gate, 'mp', axis=2, tiled=True)  72.1 us
    psum x1, blocking collectives, local(): probe_g, probe_u = lax.psum((part_gate, part_upper), 'mp')  69.8 us
    all_gather x1, waiting for transfers between devices, local(): lax.all_gather(scaled_u, 'mp', axis=2, tiled=True)  54.4 us
    dot_general x2, matrix products, update_maker(): lax.dot_general(left_side, right_side, (((0,), (0,)), ((), ())), preferre...  30.1 us
    dot_general x2, matrix products, perturbed(): base_part = jnp.dot(gathered, weight, preferred_element_type=jnp.float32)  19.6 us
    unnamed x23, local copies, waits for them, and re-layouts  15.4 us
  transfers between devices with their start and end apart: 5, of which 4 were waited for; matrix products, arithmetic and copies ran while one was open for 16% of the time, Pallas kernels for 0%

commit v1 on v0

v1 whole, which is shorter than its diff:
```python
import functools

import jax
import jax.numpy as jnp
from jax import lax
from jax.experimental import pallas as pl
from jax.experimental.pallas import tpu as pltpu
from jax.sharding import Mesh
from jax.sharding import PartitionSpec as P

bf16 = jnp.bfloat16
f32 = jnp.float32
noise_scale = 0.5
AXES = ("z", "l", "x", "h", "c")
VMEM = 56 * 1024 * 1024


def _params():
    return pltpu.CompilerParams(vmem_limit_bytes=VMEM)


def _own_mask(members, tokens):
    m = lax.broadcasted_iota(jnp.int32, (members, tokens), 0)
    t = lax.broadcasted_iota(jnp.int32, (members, tokens), 1)
    return jnp.logical_or(t == 2 * m, t == 2 * m + 1)


def _probe_kernel(tok_ref, ag_ref, au_ref, out_ref):
    tok = tok_ref[...]
    mask = _own_mask(ag_ref.shape[2], tok.shape[1])
    rows = []
    for ref in (ag_ref, au_ref):
        for r in range(ref.shape[0]):
            s = lax.dot_general(ref[r], tok, (((0,), (0,)), ((), ())), preferred_element_type=f32)
            rows.append(jnp.sum(jnp.where(mask, s, 0.0), axis=0, keepdims=True))
    out_ref[...] = jnp.concatenate(rows, axis=0)


def probes(tok_t, ag, au):
    return pl.pallas_call(
        _probe_kernel,
        out_shape=jax.ShapeDtypeStruct((2 * ag.shape[0], tok_t.shape[1]), f32),
        compiler_params=_params(),
        name="probes",
    )(tok_t, ag, au)


def _update_kernel(coeff, own_ref, oth_ref, b0_ref, b1_ref, out_ref):
    rank = b0_ref.shape[0]
    rhs = jnp.concatenate([b0_ref[r] for r in range(rank)] + [b1_ref[r] for r in range(rank)], axis=1)
    rows = []
    for ref in (own_ref, oth_ref):
        rows.append(jnp.concatenate([ref[0, s, r] for s in range(2) for r in range(rank)], axis=1))
    lhs = jnp.concatenate(rows, axis=0)
    acc = lax.dot_general(lhs, rhs, (((1,), (1,)), ((), ())), preferred_element_type=f32)
    out_ref[0] = (acc * coeff).astype(out_ref.dtype)


def update(coeff, own, oth, b0, b1):
    nx, _, rank, d, m = own.shape
    q = b0.shape[1]
    a_spec = pl.BlockSpec((1, 2, rank, d, m), lambda i: (i, 0, 0, 0, 0))
    b_spec = pl.BlockSpec((rank, q, m), lambda i: (0, 0, 0))
    return pl.pallas_call(
        functools.partial(_update_kernel, coeff),
        grid=(nx,),
        in_specs=[a_spec, a_spec, b_spec, b_spec],
        out_specs=pl.BlockSpec((1, 2 * d, q), lambda i: (i, 0, 0)),
        out_shape=jax.ShapeDtypeStruct((nx, 2 * d, q), bf16),
        compiler_params=_params(),
        cost_estimate=pl.CostEstimate(
            flops=2 * nx * 2 * d * 2 * rank * m * q,
            bytes_accessed=2 * (4 * nx * rank * d * m + 2 * rank * q * m + nx * 2 * d * q),
            transcendentals=0,
        ),
        name="update",
    )(own, oth, b0, b1)


def _hidden_kernel(tok_ref, probe_ref, wg_ref, wu_ref, bg_ref, bu_ref, out_ref, p_ref):
    rank, _, m = bg_ref.shape
    t = tok_ref.shape[1]

    @pl.when(pl.program_id(0) == 0)
    def _():
        mask = _own_mask(m, t)
        for i in range(2 * rank):
            row = (probe_ref[i : i + 1, :].astype(bf16).astype(f32)) * noise_scale
            p_ref[i * m : (i + 1) * m, :] = jnp.where(mask, jnp.broadcast_to(row, (m, t)), 0.0).astype(bf16)

    tok = tok_ref[...]
    pre = []
    for k, (w_ref, b_ref) in enumerate(((wg_ref, bg_ref), (wu_ref, bu_ref))):
        b = jnp.concatenate([b_ref[r] for r in range(rank)], axis=1)
        acc = jnp.dot(w_ref[...], tok, preferred_element_type=f32)
        acc += jnp.dot(b, p_ref[k * rank * m : (k + 1) * rank * m, :], preferred_element_type=f32)
        pre.append(acc)
    g, u = pre
    out_ref[...] = (g / (1.0 + jnp.exp(-g)) * u).astype(out_ref.dtype)


def hidden_of(tok, probe, wg, wu, bg, bu):
    d, t = tok.shape
    q = wg.shape[0]
    rank, _, m = bg.shape
    block = 304
    w_spec = pl.BlockSpec((block, d), lambda i: (i, 0))
    b_spec = pl.BlockSpec((rank, block, m), lambda i: (0, i, 0))
    return pl.pallas_call(
        _hidden_kernel,
        grid=(pl.cdiv(q, block),),
        in_specs=[
            pl.BlockSpec((d, t), lambda i: (0, 0)),
            pl.BlockSpec((2 * rank, t), lambda i: (0, 0)),
            w_spec,
            w_spec,
            b_spec,
            b_spec,
        ],
        out_specs=pl.BlockSpec((block, t), lambda i: (i, 0)),
        out_shape=jax.ShapeDtypeStruct((q, t), bf16),
        scratch_shapes=[pltpu.VMEM((2 * rank * m, t), bf16)],
        compiler_params=_params(),
        cost_estimate=pl.CostEstimate(
            flops=4 * q * t * (d + rank * m),
            bytes_accessed=2 * (2 * q * d + d * t + 2 * rank * q * m + q * t),
            transcendentals=q * t,
        ),
        name="hidden",
    )(tok, probe, wg, wu, bg, bu)


def swap(v, axis, shift=1):
    n = lax.axis_size(axis)
    return lax.ppermute(v, axis, [(i, (i + shift) % n) for i in range(n)])


def local(tokens, w_gate, w_up, a_gate, a_up, b_gate, b_up, fitness):
    members, rank, d_own = a_gate.shape
    q = w_gate.shape[1]
    pops = lax.axis_size("z") * lax.axis_size("l")
    coeff = 1.0 / (members * pops * rank) ** 0.5
    h, l, c = lax.axis_index("h"), lax.axis_index("l"), lax.axis_index("c")
    y = 2 * h + l
    at_y = (0, 2, 1, 3)
    tok_t = tokens.T
    a_t = [a.transpose(1, 2, 0) for a in (a_gate, a_up)]
    b_t = [b.transpose(1, 2, 0) for b in (b_gate, b_up)]
    cuts = ((0, 640), (640, q))

    def factors(a):
        s = (a.astype(f32) * fitness[None, None, :]).astype(bf16)
        pa = lax.ppermute(s, ("l", "h"), [(at_y[i], at_y[j]) for i, j in ((1, 0), (2, 1), (0, 2))])
        pb = lax.ppermute(s, ("l", "h"), [(at_y[i], at_y[j]) for i, j in ((3, 1), (1, 2), (2, 3))])
        mine = jnp.where(y == 1, pb, jnp.where(y == 2, pa, s))
        other = jnp.where(y < 2, pa, pb)
        both = jnp.stack([mine, other])
        own = lax.all_gather(both, "x", axis=0, tiled=False)
        return own, swap(own, "c")

    part = probes(tok_t, *a_t)
    part = part + swap(part, "c")
    part = part + swap(part, "h")
    part = part + lax.ppermute(part, "x", [(i, i ^ 1) for i in range(4)])
    part = part + lax.ppermute(part, "x", [(i, i ^ 2) for i in range(4)])

    sums = []
    for a, b in zip(a_t, b_t):
        own, oth = factors(a)
        pieces = []
        for lo, hi in cuts:
            b0 = lax.slice_in_dim(b, lo, hi, axis=1)
            b1 = swap(b0, "l")
            prod = update(coeff, own, oth, b0, b1)
            prod = prod.reshape(prod.shape[0] * prod.shape[1], hi - lo)
            pieces.append(lax.psum_scatter(prod, "z", scatter_dimension=0, tiled=True))
        sums.append(pieces)

    near = jnp.stack([tok_t, swap(tok_t, "h")])
    near = jnp.where(h == 0, near, near[::-1])
    mine = lax.all_gather(near, "x", axis=0, tiled=False)
    other = swap(mine, "c")
    tok = jnp.where(c == 0, jnp.stack([mine, other], axis=2), jnp.stack([other, mine], axis=2))
    tok = tok.reshape(-1, tok_t.shape[1])
    hidden = hidden_of(tok, part, w_gate.T, w_up.T, *b_t).T

    rows = 2 * d_own
    first = (lax.axis_index("z") * 2 + l) * rows
    news = []
    for w, pieces in zip((w_gate, w_up), sums):
        keep = lax.dynamic_slice_in_dim(w, first, rows, 0).astype(f32)
        total = jnp.concatenate(pieces, axis=1)
        total = jnp.where(c == 0, total, jnp.concatenate([total[d_own:], total[:d_own]], axis=0))
        news.append((keep + total.astype(f32)).astype(bf16))
    return hidden, news[0], news[1]


def solution(mesh):
    fine = Mesh(mesh.devices.reshape(4, 2, 4, 2, 2), AXES)
    pop, mp = ("z", "l"), ("x", "h", "c")
    return jax.shard_map(
        local,
        mesh=fine,
        in_specs=(
            P(pop, mp),
            P(None, mp),
            P(None, mp),
            P(pop, None, mp),
            P(pop, None, mp),
            P(pop, None, mp),
            P(pop, None, mp),
            P(pop),
        ),
        out_specs=(P(pop, mp), P(pop, mp), P(pop, mp)),
        check_vma=False,
    )
```

time: 595 us -> 310 us (0.52)
  waiting for transfers between devices: 411 us -> 159 us
  blocking collectives: 69.8 us -> 0 us
  matrix products: 61.2 us -> 0 us
  Pallas kernels: 0 us -> 59 us
  starting transfers between devices: 0.2 us -> 42.3 us
  local copies, waits for them, and re-layouts: 31 us -> 18.6 us
  other arithmetic: 7.45 us -> 14.1 us
    reduce_scatter x2 -> x4, waiting for transfers between devices: 283 us -> 0.07 us  [local(): pieces.append(lax.psum_scatter(prod, 'z', scatter_dimension=0, tiled=True))]
    ppermute x0 -> x16, waiting for transfers between devices: none -> 131 us  [the longest x10 111 us: swap(): return lax.ppermute(v, axis, [(i, (i + shift) % n) for i in range(n)])]
    all_gather x3, waiting for transfers between devices: 126 us -> 27.9 us  [the longest x2 27.9 us: factors(): own = lax.all_gather(both, 'x', axis=0, tiled=False)]
    psum x1 -> x0, blocking collectives: 69.8 us -> none  [local(): probe_g, probe_u = lax.psum((part_gate, part_upper), 'mp')]
    dot_general x8 -> x0, matrix products: 61.2 us -> none  [the longest x2 30.1 us: update_maker(): lax.dot_general(left_side, right_side, (((0,), (0,)), ((), ())), preferre...]
    pallas_call x0 -> x6, Pallas kernels: none -> 59 us  [the longest x4 38.8 us: update(): pl.pallas_call(functools.partial(_update_kernel, coeff), grid=(nx,), in_s...]
    ppermute x0 -> x16, starting transfers between devices: none -> 42 us  [the longest x2 20.9 us: factors(): lax.ppermute(s, ('l', 'h'), [(at_y[i], at_y[j]) for i, j in ((1, 0), (2,...]
    mul x4 -> x0, local copies, waits for them, and re-layouts: 10.8 us -> none  [perturbed(): return base_part + noise_scale * lowrank_noise.reshape(base_part.shape)]
  transfers between devices with their start and end apart: 5 -> 23, of which waited for: 4 -> 10; matrix products, arithmetic and copies ran while one was open for 16% -> 7% of each run, Pallas kernels for 0% -> 19%
where the time goes in v1:
time: 310 us; the launch traced here: 308 us
  waiting for transfers between devices  159 us (51%)
  Pallas kernels  59 us (19%)
  starting transfers between devices  42.3 us (14%)
  local copies, waits for them, and re-layouts  18.6 us (6%)
  between operations  14.4 us (5%)
  other arithmetic  14.1 us (5%)
    ppermute x10, waiting for transfers between devices, swap(): return lax.ppermute(v, axis, [(i, (i + shift) % n) for i in range(n)])  111 us
    pallas_call x4, Pallas kernels, update(): pl.pallas_call(functools.partial(_update_kernel, coeff), grid=(nx,), in_s...  38.8 us
    all_gather x2, waiting for transfers between devices, factors(): own = lax.all_gather(both, 'x', axis=0, tiled=False)  27.9 us
    ppermute x2, starting transfers between devices, factors(): lax.ppermute(s, ('l', 'h'), [(at_y[i], at_y[j]) for i, j in ((1, 0), (2,...  20.9 us
    ppermute x2, waiting for transfers between devices, factors(): lax.ppermute(s, ('l', 'h'), [(at_y[i], at_y[j]) for i, j in ((1, 0), (2,...  19.8 us
    ppermute x10, starting transfers between devices, swap(): return lax.ppermute(v, axis, [(i, (i + shift) % n) for i in range(n)])  17.5 us
    pallas_call x1, Pallas kernels, hidden_of(): pl.pallas_call(_hidden_kernel, grid=(pl.cdiv(q, block),), in_specs=[pl.Bl...  17.4 us
    unnamed x30, local copies, waits for them, and re-layouts  10.7 us
  transfers between devices with their start and end apart: 23, of which 10 were waited for; matrix products, arithmetic and copies ran while one was open for 7% of the time, Pallas kernels for 19%

profile of v1, /device:TPU:1, one launch (start us, length us, event | category | flops | bytes accessed | tf_op | source)
XLA Modules:
  0.0 307.6 jit_solution(11684842004460993003)
XLA Ops:
  7.2 1.3 multiply_convert_fusion
  8.5 0.7 collective-permute-start.11
  9.2 7.9 %collective-permute-start.12 = (bf16[4,224,256]{2,1,0:T(8,128)(2,1)S(1)}, bf16[4,224,256]{2,1,0:T(8,128)(2,1)S(1)}, u32[]{:S(2)}, u32[]{:S(2)}) collective-permute-start(bf16[4,224,256]{2,1,0:T(8,128)(2,1)S(1)} %get-tuple-element.11), channel_id=1, source_target_pairs={{16,0},{2,16},{0,2},{17,1},{3,17},{1,3},{20,4},{6,20},{4,6},{21,5}... | collective-permute-start | bytes 1376264 | tf_op jit(solution)/shard_map/ppermute | solution.py:153
  17.2 8.9 %collective-permute-done.12 = bf16[4,224,256]{2,1,0:T(8,128)(2,1)S(1)} collective-permute-done((bf16[4,224,256]{2,1,0:T(8,128)(2,1)S(1)}, bf16[4,224,256]{2,1,0:T(8,128)(2,1)S(1)}, u32[]{:S(2)}, u32[]{:S(2)}) %collective-permute-start.12) | collective-permute-done | bytes 458784 | tf_op jit(solution)/shard_map/ppermute | solution.py:153
  26.1 0.1 select_bitcast_fusion.1
  26.1 1.0 pad_maximum_fusion.1
  27.2 0.7 collective-permute-start.6
  27.9 13.0 %collective-permute-start.7 = (bf16[4,224,256]{2,1,0:T(8,128)(2,1)S(1)}, bf16[4,224,256]{2,1,0:T(8,128)(2,1)S(1)}, u32[]{:S(2)}, u32[]{:S(2)}) collective-permute-start(bf16[4,224,256]{2,1,0:T(8,128)(2,1)S(1)} %get-tuple-element.12), channel_id=1, source_target_pairs={{16,0},{2,16},{0,2},{17,1},{3,17},{1,3},{20,4},{6,20},{4,6},{21,5}... | collective-permute-start | bytes 1376264 | tf_op jit(solution)/shard_map/ppermute | solution.py:153
  40.9 10.9 %collective-permute-done.7 = bf16[4,224,256]{2,1,0:T(8,128)(2,1)S(1)} collective-permute-done((bf16[4,224,256]{2,1,0:T(8,128)(2,1)S(1)}, bf16[4,224,256]{2,1,0:T(8,128)(2,1)S(1)}, u32[]{:S(2)}, u32[]{:S(2)}) %collective-permute-start.7) | collective-permute-done | bytes 458784 | tf_op jit(solution)/shard_map/ppermute | solution.py:153
  51.8 0.1 select_bitcast_fusion.3
  51.9 1.0 pad_maximum_fusion
  52.9 0.0 all-gather.7.cloned.1.call-start
  53.0 27.9 %all-gather.11.cloned.1.call-done = bf16[8,4,224,256]{3,2,1,0:T(8,128)(2,1)} async-done(((bf16[2,4,224,256]{3,2,1,0:T(8,128)(2,1)}), bf16[8,4,224,256]{3,2,1,0:T(8,128)(2,1)}) %all-gather.11.cloned.1.call-update) | async-done | bytes 3670032 | tf_op jit(solution)/shard_map/all_gather | solution.py:158
  80.9 0.7 collective-permute-start.13
  81.6 2.7 collective-permute-start
  84.3 6.0 %collective-permute-done = bf16[224,512]{1,0:T(8,128)(2,1)S(1)} collective-permute-done((bf16[224,512]{1,0:T(8,128)(2,1)S(1)}, bf16[224,512]{1,0:T(8,128)(2,1)S(1)}, u32[]{:S(2)}, u32[]{:S(2)}) %collective-permute-start) | collective-permute-done | bytes 229408 | tf_op jit(solution)/shard_map/ppermute | solution.py:135
  90.4 0.9 reverse_select_fusion
  91.2 0.0 reduce-scatter.9.cloned.1.call-start
  91.3 0.1 slice.36.b0_ref
  91.4 1.3 collective-permute-start.14
  92.7 28.4 %collective-permute-done.14.b1_ref = bf16[4,640,256]{2,1,0:T(8,128)(2,1)S(1)} collective-permute-done((bf16[4,640,256]{2,1,0:T(8,128)(2,1)S(1)}, bf16[4,640,256]{2,1,0:T(8,128)(2,1)S(1)}, u32[]{:S(2)}, u32[]{:S(2)}) %collective-permute-start.14) | collective-permute-done | bytes 1310752 | tf_op jit(solution)/shard_map/ppermute | solution.py:135
  121.1 1.1 copy-done.9
  122.2 9.8 %update.6 = bf16[4,448,640]{2,1,0:T(8,128)(2,1)} custom-call(bf16[4,2,4,224,256]{4,3,2,1,0:T(8,128)(2,1)} %bitcast.55, bf16[4,2,4,224,256]{4,3,2,1,0:T(8,128)(2,1)} %collective-permute-done.13.oth_ref, bf16[4,640,256]{2,1,0:T(8,128)(2,1)} %copy-done.4, bf16[4,640,256]{2,1,0:T(8,128)(2,1)} %copy-done.9), custom_call_target="tpu_custom_call" | custom-call | flops 4697620480 | bytes 12255232 | tf_op jit(solution)/shard_map/update/pallas_call | solution.py:64
  132.0 1.6 collective-permute-start.8
  133.7 0.1 slice.32.b0_ref
  133.8 1.3 collective-permute-start.9
  135.1 29.2 %collective-permute-done.9.b1_ref = bf16[4,640,256]{2,1,0:T(8,128)(2,1)S(1)} collective-permute-done((bf16[4,640,256]{2,1,0:T(8,128)(2,1)S(1)}, bf16[4,640,256]{2,1,0:T(8,128)(2,1)S(1)}, u32[]{:S(2)}, u32[]{:S(2)}) %collective-permute-start.9) | collective-permute-done | bytes 1310752 | tf_op jit(solution)/shard_map/ppermute | solution.py:135
  164.3 1.1 copy-done.10
  165.4 9.7 %update.4 = bf16[4,448,640]{2,1,0:T(8,128)(2,1)} custom-call(bf16[4,2,4,224,256]{4,3,2,1,0:T(8,128)(2,1)} %bitcast.58, bf16[4,2,4,224,256]{4,3,2,1,0:T(8,128)(2,1)} %collective-permute-done.8.oth_ref, bf16[4,640,256]{2,1,0:T(8,128)(2,1)} %copy-done.5, bf16[4,640,256]{2,1,0:T(8,128)(2,1)} %copy-done.10), custom_call_target="tpu_custom_call" | custom-call | flops 4697620480 | bytes 12255232 | tf_op jit(solution)/shard_map/update/pallas_call | solution.py:64
  175.2 1.4 slice.37.b0_ref
  176.6 1.4 collective-permute-start.15
  178.0 24.0 %collective-permute-done.15.b1_ref = bf16[4,544,256]{2,1,0:T(8,128)(2,1)S(1)} collective-permute-done((bf16[4,544,256]{2,1,0:T(8,128)(2,1)S(1)}, bf16[4,544,256]{2,1,0:T(8,128)(2,1)S(1)}, u32[]{:S(2)}, u32[]{:S(2)}) %collective-permute-start.15) | collective-permute-done | bytes 1114144 | tf_op jit(solution)/shard_map/ppermute | solution.py:135
  202.0 1.0 copy-done.12
  203.0 9.7 %update.7 = bf16[4,448,544]{2,1,0:T(8,128)(2,1)} custom-call(bf16[4,2,4,224,256]{4,3,2,1,0:T(8,128)(2,1)} %bitcast.56, bf16[4,2,4,224,256]{4,3,2,1,0:T(8,128)(2,1)} %collective-permute-done.13.oth_ref, bf16[4,544,256]{2,1,0:T(8,128)(2,1)} %copy-done.7, bf16[4,544,256]{2,1,0:T(8,128)(2,1)} %copy-done.12), custom_call_target="tpu_custom_call" | custom-call | flops 3992977408 | bytes 11517952 | tf_op jit(solution)/shard_map/update/pallas_call | solution.py:64
  212.8 0.1 slice.33.b0_ref
  212.9 1.5 collective-permute-start.10
  214.4 1.7 collective-permute-start.1
  216.0 21.5 %collective-permute-done.10.b1_ref = bf16[4,544,256]{2,1,0:T(8,128)(2,1)S(1)} collective-permute-done((bf16[4,544,256]{2,1,0:T(8,128)(2,1)S(1)}, bf16[4,544,256]{2,1,0:T(8,128)(2,1)S(1)}, u32[]{:S(2)}, u32[]{:S(2)}) %collective-permute-start.10) | collective-permute-done | bytes 1114144 | tf_op jit(solution)/shard_map/ppermute | solution.py:135
  237.6 1.0 copy-done.11
  238.6 9.5 %update.5 = bf16[4,448,544]{2,1,0:T(8,128)(2,1)} custom-call(bf16[4,2,4,224,256]{4,3,2,1,0:T(8,128)(2,1)} %bitcast.59, bf16[4,2,4,224,256]{4,3,2,1,0:T(8,128)(2,1)} %collective-permute-done.8.oth_ref, bf16[4,544,256]{2,1,0:T(8,128)(2,1)} %copy-done.6, bf16[4,544,256]{2,1,0:T(8,128)(2,1)} %copy-done.11), custom_call_target="tpu_custom_call" | custom-call | flops 3992977408 | bytes 11517952 | tf_op jit(solution)/shard_map/update/pallas_call | solution.py:64
  248.1 2.8 probes.1
  250.9 2.4 collective-permute-start.2
  253.3 1.0 collective-permute-done.2
  254.3 0.7 add.36
  255.1 2.9 collective-permute-start.3
  258.0 1.1 collective-permute-done.3
  259.2 0.8 collective-permute-start.4
  260.0 2.0 constant_dynamic-slice_fusion
  262.0 1.4 collective-permute-start.5
  263.4 2.0 constant_dynamic-slice_fusion.1
  265.4 1.6 copy.20
  266.9 1.5 copy.19
  268.5 0.6 add.39.probe_ref
  269.1 5.4 %maximum_select_fusion = bf16[4,2,2,224,512]{4,3,2,1,0:T(8,128)(2,1)} fusion(bf16[4,2,1,224,512]{4,3,2,1,0:T(8,128)(2,1)} %bitcast.6, bf16[4,2,1,224,512]{4,3,2,1,0:T(8,128)(2,1)} %bitcast.47, pred[]{:T(512)S(6)} %eq.16), kind=kLoop, calls=%fused_computation | loop fusion | flops 5505024 | bytes 7340033 | tf_op jit(solution)/shard_map/jit(_where)/select_n | solution.py:183
  274.5 17.4 %hidden.1 = bf16[1184,512]{1,0:T(8,128)(2,1)} custom-call(bf16[3584,512]{1,0:T(8,128)(2,1)} %bitcast.33, f32[8,512]{1,0:T(8,128)} %add.39.probe_ref, bf16[1184,3584]{1,0:T(8,128)(2,1)} %bitcast.52, bf16[1184,3584]{1,0:T(8,128)(2,1)} %bitcast.53, bf16[4,1184,256]{2,1,0:T(8,128)(2,1)} %bitcast.34, bf16[4,1184,256]{2,1,0:T(8,128)(2,1)} %bitcast.38), custom_call_target="tpu_custom_call" | custom-call | flops 11173625856 | bytes 26705920 | tf_op jit(solution)/shard_map/hidden/pallas_call | solution.py:109
  291.8 1.1 constant_dynamic-update-slice_fusion.3
  293.0 1.1 constant_dynamic-update-slice_fusion.1
  294.1 1.1 constant_dynamic-update-slice_fusion.2
  295.3 0.1 fusion
  295.4 1.1 constant_dynamic-update-slice_fusion
  296.5 0.1 fusion.1
  296.6 1.2 copy-done
  297.8 1.5 add_convert_fusion
  299.3 1.5 add_convert_fusion.1
  (49 shorter events, 0.5 us)
Async XLA Ops:
  7.2 73.7 %all-gather.11.cloned.1.call-start = ((), (), s32[]{:S(2)}) async-start(), calls=%async_computation.10 | async-start | bytes 4587520 | tf_op jit(solution)/shard_map/all_gather | solution.py:158
  8.5 8.6 %collective-permute-start.11 = (bf16[4,224,256]{2,1,0:T(8,128)(2,1)S(1)}, bf16[4,224,256]{2,1,0:T(8,128)(2,1)S(1)}, u32[]{:S(2)}, u32[]{:S(2)}) collective-permute-start(bf16[4,224,256]{2,1,0:T(8,128)(2,1)S(1)} %get-tuple-element.11), channel_id=1, source_target_pairs={{18,16},{16,2},{2,18},{19,17},{17,3},{3,19},{22,20},{20,6},{6,22},... | collective-permute-start | bytes 1376264 | tf_op jit(solution)/shard_map/ppermute | solution.py:154
  9.2 16.8 %collective-permute-start.12 = (bf16[4,224,256]{2,1,0:T(8,128)(2,1)S(1)}, bf16[4,224,256]{2,1,0:T(8,128)(2,1)S(1)}, u32[]{:S(2)}, u32[]{:S(2)}) collective-permute-start(bf16[4,224,256]{2,1,0:T(8,128)(2,1)S(1)} %get-tuple-element.11), channel_id=1, source_target_pairs={{16,0},{2,16},{0,2},{17,1},{3,17},{1,3},{20,4},{6,20},{4,6},{21,5}... | collective-permute-start | bytes 1376264 | tf_op jit(solution)/shard_map/ppermute | solution.py:153
  27.2 104.9 %all-gather.9.cloned.1.call-start = ((), (), s32[]{:S(2)}) async-start(), calls=%async_computation.9 | async-start | bytes 4587520 | tf_op jit(solution)/shard_map/all_gather | solution.py:158
  27.2 13.7 %collective-permute-start.6 = (bf16[4,224,256]{2,1,0:T(8,128)(2,1)S(1)}, bf16[4,224,256]{2,1,0:T(8,128)(2,1)S(1)}, u32[]{:S(2)}, u32[]{:S(2)}) collective-permute-start(bf16[4,224,256]{2,1,0:T(8,128)(2,1)S(1)} %get-tuple-element.12), channel_id=1, source_target_pairs={{18,16},{16,2},{2,18},{19,17},{17,3},{3,19},{22,20},{20,6},{6,22},... | collective-permute-start | bytes 1376264 | tf_op jit(solution)/shard_map/ppermute | solution.py:154
  27.9 23.9 %collective-permute-start.7 = (bf16[4,224,256]{2,1,0:T(8,128)(2,1)S(1)}, bf16[4,224,256]{2,1,0:T(8,128)(2,1)S(1)}, u32[]{:S(2)}, u32[]{:S(2)}) collective-permute-start(bf16[4,224,256]{2,1,0:T(8,128)(2,1)S(1)} %get-tuple-element.12), channel_id=1, source_target_pairs={{16,0},{2,16},{0,2},{17,1},{3,17},{1,3},{20,4},{6,20},{4,6},{21,5}... | collective-permute-start | bytes 1376264 | tf_op jit(solution)/shard_map/ppermute | solution.py:153
  51.9 29.7 %copy-start.8 = (bf16[512,224]{0,1:T(8,128)(2,1)S(1)}, bf16[512,224]{0,1:T(8,128)(2,1)}, u32[]{:S(2)}) copy-start(bf16[512,224]{0,1:T(8,128)(2,1)} %param.8) | copy-start | bytes 688132
  52.9 38.4 %copy-start.3 = (bf16[256,4,1184]{0,2,1:T(8,128)(2,1)S(1)}, bf16[256,4,1184]{0,2,1:T(8,128)(2,1)}, u32[]{:S(2)}) copy-start(bf16[256,4,1184]{0,2,1:T(8,128)(2,1)} %param.14) | copy-start | bytes 7274500
  52.9 161.4 %all-gather.7.cloned.1.call-start = ((), (), s32[]{:S(2)}) async-start(), calls=%async_computation.8 | async-start | bytes 2293760 | tf_op jit(solution)/shard_map/all_gather | solution.py:181
  80.9 40.2 %collective-permute-start.13 = (bf16[4,2,4,224,256]{4,3,2,1,0:T(8,128)(2,1)}, bf16[4,2,4,224,256]{4,3,2,1,0:T(8,128)(2,1)}, u32[]{:S(2)}, u32[]{:S(2)}) collective-permute-start(bf16[4,2,4,224,256]{4,3,2,1,0:T(8,128)(2,1)} %bitcast.54), channel_id=1, source_target_pairs={{0,1},{1,0},{2,3},{3,2},{4,5},{5,4},{6,7},{7,6},{8,9},{9,8},{10,11... | collective-permute-start | bytes 11010056 | tf_op jit(solution)/shard_map/ppermute | solution.py:135
  81.6 8.7 %collective-permute-start = (bf16[224,512]{1,0:T(8,128)(2,1)S(1)}, bf16[224,512]{1,0:T(8,128)(2,1)S(1)}, u32[]{:S(2)}, u32[]{:S(2)}) collective-permute-start(bf16[224,512]{1,0:T(8,128)(2,1)S(1)} %bitcast.49), channel_id=1, source_target_pairs={{0,2},{2,0},{1,3},{3,1},{4,6},{6,4},{5,7},{7,5},{8,10},{10,8},{9,1... | collective-permute-start | bytes 688136 | tf_op jit(solution)/shard_map/ppermute | solution.py:135
  91.2 200.6 %reduce-scatter.9.cloned.1.call-start = ((), (), s32[]{:S(2)}) async-start(), calls=%async_computation.6 | async-start | bytes 2867200 | tf_op jit(solution)/shard_map/reduce_scatter | solution.py:176
  91.4 29.7 %copy-start.4 = (bf16[4,640,256]{2,1,0:T(8,128)(2,1)}, bf16[4,640,256]{2,1,0:T(8,128)(2,1)S(1)}, u32[]{:S(2)}) copy-start(bf16[4,640,256]{2,1,0:T(8,128)(2,1)S(1)} %slice.36.b0_ref) | copy-start | bytes 3932164
  91.4 29.7 %collective-permute-start.14 = (bf16[4,640,256]{2,1,0:T(8,128)(2,1)S(1)}, bf16[4,640,256]{2,1,0:T(8,128)(2,1)S(1)}, u32[]{:S(2)}, u32[]{:S(2)}) collective-permute-start(bf16[4,640,256]{2,1,0:T(8,128)(2,1)S(1)} %slice.36.b0_ref), channel_id=1, source_target_pairs={{0,16},{16,0},{1,17},{17,1},{2,18},{18,2},{3,19},{19,3},{4,20},{20... | collective-permute-start | bytes 3932168 | tf_op jit(solution)/shard_map/ppermute | solution.py:135
  121.1 1.1 copy-start.9
  122.2 11.5 %copy-start.2 = (bf16[256,4,1184]{0,2,1:T(8,128)(2,1)S(1)}, bf16[256,4,1184]{0,2,1:T(8,128)(2,1)}, u32[]{:S(2)}) copy-start(bf16[256,4,1184]{0,2,1:T(8,128)(2,1)} %param.13) | copy-start | bytes 7274500
  132.0 161.0 %reduce-scatter.5.cloned.1.call-start = ((), (), s32[]{:S(2)}) async-start(), calls=%async_computation.4 | async-start | bytes 2867200 | tf_op jit(solution)/shard_map/reduce_scatter | solution.py:176
  132.0 32.2 %collective-permute-start.8 = (bf16[4,2,4,224,256]{4,3,2,1,0:T(8,128)(2,1)}, bf16[4,2,4,224,256]{4,3,2,1,0:T(8,128)(2,1)}, u32[]{:S(2)}, u32[]{:S(2)}) collective-permute-start(bf16[4,2,4,224,256]{4,3,2,1,0:T(8,128)(2,1)} %bitcast.57), channel_id=1, source_target_pairs={{0,1},{1,0},{2,3},{3,2},{4,5},{5,4},{6,7},{7,6},{8,9},{9,8},{10,11... | collective-permute-start | bytes 11010056 | tf_op jit(solution)/shard_map/ppermute | solution.py:135
  133.8 30.5 %copy-start.5 = (bf16[4,640,256]{2,1,0:T(8,128)(2,1)}, bf16[4,640,256]{2,1,0:T(8,128)(2,1)S(1)}, u32[]{:S(2)}) copy-start(bf16[4,640,256]{2,1,0:T(8,128)(2,1)S(1)} %slice.32.b0_ref) | copy-start | bytes 3932164
  133.8 30.5 %collective-permute-start.9 = (bf16[4,640,256]{2,1,0:T(8,128)(2,1)S(1)}, bf16[4,640,256]{2,1,0:T(8,128)(2,1)S(1)}, u32[]{:S(2)}, u32[]{:S(2)}) collective-permute-start(bf16[4,640,256]{2,1,0:T(8,128)(2,1)S(1)} %slice.32.b0_ref), channel_id=1, source_target_pairs={{0,16},{16,0},{1,17},{17,1},{2,18},{18,2},{3,19},{19,3},{4,20},{20... | collective-permute-start | bytes 3932168 | tf_op jit(solution)/shard_map/ppermute | solution.py:135
  164.3 1.1 copy-start.10
  175.2 118.9 %reduce-scatter.11.cloned.1.call-start = ((), (), s32[]{:S(2)}) async-start(), calls=%async_computation.7 | async-start | bytes 2867200 | tf_op jit(solution)/shard_map/reduce_scatter | solution.py:176
  176.6 25.4 %copy-start.7 = (bf16[4,544,256]{2,1,0:T(8,128)(2,1)}, bf16[4,544,256]{2,1,0:T(8,128)(2,1)S(1)}, u32[]{:S(2)}) copy-start(bf16[4,544,256]{2,1,0:T(8,128)(2,1)S(1)} %slice.37.b0_ref) | copy-start | bytes 3342340
  176.6 25.4 %collective-permute-start.15 = (bf16[4,544,256]{2,1,0:T(8,128)(2,1)S(1)}, bf16[4,544,256]{2,1,0:T(8,128)(2,1)S(1)}, u32[]{:S(2)}, u32[]{:S(2)}) collective-permute-start(bf16[4,544,256]{2,1,0:T(8,128)(2,1)S(1)} %slice.37.b0_ref), channel_id=1, source_target_pairs={{0,16},{16,0},{1,17},{17,1},{2,18},{18,2},{3,19},{19,3},{4,20},{20... | collective-permute-start | bytes 3342344 | tf_op jit(solution)/shard_map/ppermute | solution.py:135
  202.0 1.0 copy-start.12
  212.8 82.6 %reduce-scatter.7.cloned.1.call-start = ((), (), s32[]{:S(2)}) async-start(), calls=%async_computation.5 | async-start | bytes 2867200 | tf_op jit(solution)/shard_map/reduce_scatter | solution.py:176
  212.9 24.7 %copy-start.6 = (bf16[4,544,256]{2,1,0:T(8,128)(2,1)}, bf16[4,544,256]{2,1,0:T(8,128)(2,1)S(1)}, u32[]{:S(2)}) copy-start(bf16[4,544,256]{2,1,0:T(8,128)(2,1)S(1)} %slice.33.b0_ref) | copy-start | bytes 3342340
  212.9 24.7 %collective-permute-start.10 = (bf16[4,544,256]{2,1,0:T(8,128)(2,1)S(1)}, bf16[4,544,256]{2,1,0:T(8,128)(2,1)S(1)}, u32[]{:S(2)}, u32[]{:S(2)}) collective-permute-start(bf16[4,544,256]{2,1,0:T(8,128)(2,1)S(1)} %slice.33.b0_ref), channel_id=1, source_target_pairs={{0,16},{16,0},{1,17},{17,1},{2,18},{18,2},{3,19},{19,3},{4,20},{20... | collective-permute-start | bytes 3342344 | tf_op jit(solution)/shard_map/ppermute | solution.py:135
  214.4 54.7 %collective-permute-start.1 = (bf16[4,2,224,512]{3,2,1,0:T(8,128)(2,1)}, bf16[4,2,224,512]{3,2,1,0:T(8,128)(2,1)}, u32[]{:S(2)}, u32[]{:S(2)}) collective-permute-start(bf16[4,2,224,512]{3,2,1,0:T(8,128)(2,1)} %bitcast.46), channel_id=1, source_target_pairs={{0,1},{1,0},{2,3},{3,2},{4,5},{5,4},{6,7},{7,6},{8,9},{9,8},{10,11... | collective-permute-start | bytes 5505032 | tf_op jit(solution)/shard_map/ppermute | solution.py:135
  237.6 1.0 copy-start.11
  250.9 3.5 %collective-permute-start.2 = (f32[8,512]{1,0:T(8,128)}, f32[8,512]{1,0:T(8,128)S(1)}, u32[]{:S(2)}, u32[]{:S(2)}) collective-permute-start(f32[8,512]{1,0:T(8,128)} %probes.1), channel_id=1, source_target_pairs={{0,1},{1,0},{2,3},{3,2},{4,5},{5,4},{6,7},{7,6},{8,9},{9,8},{10,11... | collective-permute-start | bytes 49160 | tf_op jit(solution)/shard_map/ppermute | solution.py:135
  255.1 4.1 %collective-permute-start.3 = (f32[8,512]{1,0:T(8,128)S(1)}, f32[8,512]{1,0:T(8,128)S(1)}, u32[]{:S(2)}, u32[]{:S(2)}) collective-permute-start(f32[8,512]{1,0:T(8,128)S(1)} %add.36), channel_id=1, source_target_pairs={{0,2},{2,0},{1,3},{3,1},{4,6},{6,4},{5,7},{7,5},{8,10},{10,8},{9,1... | collective-permute-start | bytes 49160 | tf_op jit(solution)/shard_map/ppermute | solution.py:135
  259.2 2.8 collective-permute-start.4
  262.0 6.5 %collective-permute-start.5 = (f32[8,512]{1,0:T(8,128)S(1)}, f32[8,512]{1,0:T(8,128)S(1)}, u32[]{:S(2)}, u32[]{:S(2)}) collective-permute-start(f32[8,512]{1,0:T(8,128)S(1)} %add.38), channel_id=1, source_target_pairs={{0,8},{4,12},{8,0},{12,4},{1,9},{5,13},{9,1},{13,5},{2,10},{6,14},... | collective-permute-start | bytes 49160 | tf_op jit(solution)/shard_map/ppermute | solution.py:165
  296.5 1.3 copy-start
  297.8 1.5 copy-start.1
Sparse Core Ops, SparseCore 0:
  27.3 53.5 all-gather.10
  83.1 44.1 all-gather.8
  129.6 28.9 all-gather.6
  160.8 31.5 reduce-scatter.8
  194.8 31.0 reduce-scatter.4
  228.2 31.0 reduce-scatter.10
  261.9 31.0 reduce-scatter.6

commit v2 on v0

v2 whole, which is shorter than its diff:
```python
import functools

import jax
import jax.numpy as jnp
from jax import lax
from jax.experimental import pallas as pl
from jax.experimental.pallas import tpu as pltpu
from jax.sharding import Mesh
from jax.sharding import PartitionSpec as P

bf16 = jnp.bfloat16
f32 = jnp.float32
noise_scale = 0.5
AXES = ("z", "l", "x", "h", "c")
RING = 4
VMEM = 58 * 1024 * 1024
NT = (((1,), (1,)), ((), ()))
TN = (((0,), (0,)), ((), ()))


def _call(kernel, name, flops=0, moved=0, **kw):
    return pl.pallas_call(
        kernel,
        name=name,
        compiler_params=pltpu.CompilerParams(vmem_limit_bytes=VMEM),
        cost_estimate=pl.CostEstimate(flops=flops, bytes_accessed=moved, transcendentals=0),
        **kw,
    )


def _any(n):
    return [pl.BlockSpec(memory_space=pl.ANY)] * n


FULL = pl.BlockSpec(memory_space=pltpu.VMEM)
SCALARS = pl.BlockSpec(memory_space=pltpu.SMEM)


def swap(v, axis, shift=1):
    n = lax.axis_size(axis)
    return lax.ppermute(v, axis, [(i, (i + shift) % n) for i in range(n)])


def tie(v, *after):
    return _call(
        lambda *refs: None,
        "tie",
        in_specs=_any(1 + len(after)),
        out_specs=pl.BlockSpec(memory_space=pl.ANY),
        out_shape=jax.ShapeDtypeStruct(v.shape, v.dtype),
        input_output_aliases={0: 0},
    )(v, *after)


def _own_mask(members, tokens):
    m = lax.broadcasted_iota(jnp.int32, (members, tokens), 0)
    t = lax.broadcasted_iota(jnp.int32, (members, tokens), 1)
    return jnp.logical_or(t == 2 * m, t == 2 * m + 1)


def _pack_kernel(tok_ref, ag_ref, au_ref, fit_ref, sg_ref, su_ref, pay_ref):
    rank, d, m = ag_ref.shape
    tok = tok_ref[...]
    t = tok.shape[1]
    fit = fit_ref[...]
    mask = _own_mask(m, t)
    rows = []
    for a_ref, s_ref in ((ag_ref, sg_ref), (au_ref, su_ref)):
        for r in range(rank):
            a = a_ref[r]
            s_ref[r * d : (r + 1) * d, :] = (a.astype(f32) * fit).astype(bf16)
            s = lax.dot_general(a, tok, TN, preferred_element_type=f32)
            rows.append(jnp.sum(jnp.where(mask, s, 0.0), axis=0, keepdims=True))
    part = jnp.concatenate(rows, axis=0)
    high = part.astype(bf16)
    low = (part - high.astype(f32)).astype(bf16)
    at = 0
    for v in (tok, jnp.concatenate([high, low], axis=0)):
        for lo in range(0, t, m):
            pay_ref[at : at + v.shape[0], :] = v[:, lo : lo + m]
            at += v.shape[0]


def pack(tok_t, ag, au, fit):
    rank, d, m = ag.shape
    t = tok_t.shape[1]
    pay = (d + 4 * rank) * (t // m)
    return _call(
        _pack_kernel,
        "pack",
        flops=4 * rank * d * m * t,
        moved=8 * rank * d * m,
        in_specs=[FULL] * 4,
        out_specs=[FULL] * 3,
        out_shape=[jax.ShapeDtypeStruct((n, m), bf16) for n in (rank * d, rank * d, pay)],
    )(tok_t, ag, au, fit)


def _pick_kernel(y_ref, s_ref, pa_ref, pb_ref, out_ref):
    n = s_ref.shape[0]
    y = y_ref[0]
    for where, at, ref in (
        (y == 1, 0, pb_ref),
        (y == 2, 0, pa_ref),
        (jnp.logical_or(y == 0, y == 3), 0, s_ref),
        (y < 2, n, pa_ref),
        (y >= 2, n, pb_ref),
    ):

        @pl.when(where)
        def _():
            out_ref[at : at + n, :] = ref[...]


def pick(y, s, pa, pb):
    return _call(
        _pick_kernel,
        "pick",
        moved=8 * s.size,
        in_specs=[SCALARS, FULL, FULL, FULL],
        out_specs=FULL,
        out_shape=jax.ShapeDtypeStruct((2 * s.shape[0], s.shape[1]), s.dtype),
    )(y, s, pa, pb)


ORDER = (2, 1, 3, 0)


def _update_kernel(coeff, slabs, nb, nafter, block_ref, *refs):
    a_refs, b_refs = refs[:RING], refs[RING : RING + nb]
    pp_ref, pm_ref, rp_ref, rm_ref, own_ref, lhs_ref, rhs_ref = refs[RING + nb + nafter :]
    rank, q, m = b_refs[0].shape
    d = lhs_ref.shape[0]
    n = d // 2
    i = pl.program_id(0)

    @pl.when(i == 0)
    def _():
        for j, ref in enumerate(b_refs):
            row, col = (j % 2) * q, (j // 2) * rank * m
            for r in range(rank):
                rhs_ref[row : row + q, col + r * m : col + (r + 1) * m] = ref[r]

    for j, ref in enumerate(a_refs):

        @pl.when(block_ref[i] == j)
        def _():
            for k in range(slabs):
                lhs_ref[:, k * m : (k + 1) * m] = ref[k * d : (k + 1) * d, :]

    acc = lax.dot_general(lhs_ref[...], rhs_ref[...], NT, preferred_element_type=f32)
    acc = (acc * coeff).astype(bf16)

    @pl.when(i == 0)
    def _():
        pp_ref[:n, :] = acc[:n]
        pm_ref[:n, :] = acc[n:]

    @pl.when(i == 1)
    def _():
        pp_ref[n:, :] = acc[n:]
        rp_ref[...] = acc[:n]

    @pl.when(i == 2)
    def _():
        pm_ref[n:, :] = acc[:n]
        rm_ref[...] = acc[n:]

    @pl.when(i == 3)
    def _():
        own_ref[...] = acc


def update(coeff, block, factors, seconds, *after):
    rank, q, m = seconds[0].shape
    slabs = rank * len(seconds) // 2
    d = factors[0].shape[0] // slabs
    wide = 2 * q

    def once(shape):
        return pl.BlockSpec(shape, lambda i, w: (0,) * len(shape), pipeline_mode=pl.Buffered(1))

    def kept(n):
        return pl.BlockSpec((n, wide), lambda i, w: (0, 0))

    sizes = (d, d, d // 2, d // 2, d)
    return _call(
        functools.partial(_update_kernel, coeff, slabs, len(seconds), len(after)),
        "update",
        flops=2 * RING * d * slabs * m * wide,
        moved=2 * (RING * slabs * d * m + slabs * m * wide + RING * d * wide),
        grid_spec=pltpu.PrefetchScalarGridSpec(
            num_scalar_prefetch=1,
            grid=(RING,),
            in_specs=[once(f.shape) for f in factors] + [once(b.shape) for b in seconds] + _any(len(after)),
            out_specs=[kept(n) for n in sizes],
            scratch_shapes=[pltpu.VMEM((d, slabs * m), bf16), pltpu.VMEM((wide, slabs * m), bf16)],
        ),
        out_shape=[jax.ShapeDtypeStruct((n, wide), bf16) for n in sizes],
    )(block, *factors, *seconds, *after)


def over_z(pp, pm, rp, rm, own):
    n = rp.shape[0]
    gp, gm = swap(pp, "z", 1), swap(pm, "z", -1)
    fp = swap(rp + gp[:n], "z", 1)
    fm = swap(rm + gm[:n], "z", -1)
    own = own.astype(f32)
    first = own[:n] + gm[n:].astype(f32) + fp.astype(f32)
    second = own[n:] + gp[n:].astype(f32) + fm.astype(f32)
    return jnp.concatenate([first, second], axis=0)


def _tokens_kernel(at_ref, *refs):
    ins, (tok_ref, part_ref) = refs[:RING], refs[RING:]
    _, _, d, t = tok_ref.shape
    m = ins[0].shape[2]
    x, h = at_ref[0], at_ref[1]
    wide = t // m
    total = None
    for j, ref in enumerate(ins):
        for s in range(2):
            rows = [ref[s, i * d : (i + 1) * d, :] for i in range(wide)]
            tok_ref[lax.rem(x + RING - j, RING), h if s == 0 else 1 - h] = jnp.concatenate(rows, axis=1)
            last = ref[s, wide * d :, :].astype(f32)
            n = last.shape[0] // wide
            both = jnp.concatenate([last[i * n : (i + 1) * n] for i in range(wide)], axis=1)
            value = both[: n // 2] + both[n // 2 :]
            total = value if total is None else total + value
    part_ref[...] = total


def tokens_of(at, parts, d, t, probes):
    return _call(
        _tokens_kernel,
        "tokens",
        moved=16 * parts[0].size,
        in_specs=[SCALARS] + [FULL] * RING,
        out_specs=[FULL] * 2,
        out_shape=[jax.ShapeDtypeStruct((RING, 2, d, t), bf16), jax.ShapeDtypeStruct((probes, t), f32)],
    )(at, *parts)


def _hidden_kernel(c_ref, mine_ref, other_ref, p0_ref, p1_ref, wg_ref, wu_ref, bg_ref, bu_ref, *refs):
    out_ref, tok_ref, p_ref = refs[-3:]
    rank, _, m = bg_ref.shape
    nx, nh, d, t = mine_ref.shape

    @pl.when(pl.program_id(0) == 0)
    def _():
        c = c_ref[0]
        for ref, core in ((mine_ref, c), (other_ref, 1 - c)):
            for i in range(nx):
                for j in range(nh):
                    row = pl.multiple_of((2 * (nh * i + j) + core) * d, d)
                    tok_ref[pl.ds(row, d), :] = ref[i, j]
        mask = _own_mask(m, t)
        probe = (p0_ref[...] + p1_ref[...]).astype(bf16).astype(f32) * noise_scale
        for i in range(2 * rank):
            row = jnp.broadcast_to(probe[i : i + 1, :], (m, t))
            p_ref[i * m : (i + 1) * m, :] = jnp.where(mask, row, 0.0).astype(bf16)

    pre = []
    for k, (w_ref, b_ref) in enumerate(((wg_ref, bg_ref), (wu_ref, bu_ref))):
        b = jnp.concatenate([b_ref[r] for r in range(rank)], axis=1)
        acc = jnp.dot(w_ref[...], tok_ref[...], preferred_element_type=f32)
        acc += jnp.dot(b, p_ref[k * rank * m : (k + 1) * rank * m, :], preferred_element_type=f32)
        pre.append(acc)
    g, u = pre
    out_ref[...] = (g / (1.0 + jnp.exp(-g)) * u).astype(out_ref.dtype)


def hidden_of(c, mine, other, p0, p1, wg, wu, bg, bu, *after):
    t = mine.shape[3]
    q, d = wg.shape
    rank, _, m = bg.shape
    block = 304
    w_spec = pl.BlockSpec((block, d), lambda i: (i, 0))
    b_spec = pl.BlockSpec((rank, block, m), lambda i: (0, i, 0))
    t_spec = pl.BlockSpec(mine.shape, lambda i: (0, 0, 0, 0), pipeline_mode=pl.Buffered(1))
    p_spec = pl.BlockSpec(p0.shape, lambda i: (0, 0))
    return _call(
        _hidden_kernel,
        "hidden",
        flops=4 * q * t * (d + rank * m),
        moved=2 * (2 * q * d + d * t + 2 * rank * q * m + q * t),
        grid=(pl.cdiv(q, block),),
        in_specs=[SCALARS, t_spec, t_spec, p_spec, p_spec, w_spec, w_spec, b_spec, b_spec] + _any(len(after)),
        out_specs=pl.BlockSpec((block, t), lambda i: (i, 0)),
        out_shape=jax.ShapeDtypeStruct((q, t), bf16),
        scratch_shapes=[pltpu.VMEM((d, t), bf16), pltpu.VMEM((2 * rank * m, t), bf16)],
    )(c, mine, other, p0, p1, wg, wu, bg, bu, *after)


def local(tokens, w_gate, w_up, a_gate, a_up, b_gate, b_up, fitness):
    members, rank, d = a_gate.shape
    q = w_gate.shape[1]
    coeff = 1.0 / (members * lax.axis_size("z") * lax.axis_size("l") * rank) ** 0.5
    z, l, x, h, c = (lax.axis_index(a) for a in AXES)
    tok_t = tokens.T
    ag_t, au_t = (a.transpose(1, 2, 0) for a in (a_gate, a_up))
    bg, bu = (b.transpose(1, 2, 0) for b in (b_gate, b_up))
    block = (x - z - jnp.array(ORDER, jnp.int32)) % RING

    sg, su, pay = pack(tok_t, ag_t, au_t, fitness[None, :])
    bu_c, bg_c = swap(bu, "c"), swap(bg, "c")

    def round_x(v):
        return [v] + [swap(v, "x", k) for k in range(1, RING)]

    su_x = round_x(su)
    so_x = round_x(tie(swap(su, "h"), *su_x[1:]))
    at_y = (0, 2, 1, 3)
    pa, pb = (
        lax.ppermute(sg, ("l", "h"), [(at_y[i], at_y[j]) for i, j in pairs])
        for pairs in (((1, 0), (2, 1), (0, 2)), ((3, 1), (1, 2), (2, 3)))
    )
    both = pick((2 * h + l).reshape(1), sg, pa, pb)
    bg_far = swap(tie(bg, both), "l")
    bg_far_c = swap(bg_far, "c")
    sg_x = round_x(tie(both, *so_x[1:]))
    pays = tie(jnp.stack([pay, swap(pay, "h")]), *sg_x[1:])
    tok, part = tokens_of(jnp.stack([x, h]), round_x(pays), d, tok_t.shape[1], 2 * rank)

    ua = update(coeff, block, su_x, [bu, bu_c])
    ub = update(coeff, block, so_x, [bu, bu_c], ua[-1])
    gg = update(coeff, block, sg_x, [bg, bg_c, bg_far, bg_far_c], ub[-1])
    hidden = hidden_of(
        c.reshape(1), tok, swap(tok, "c"), part, swap(part, "c"), w_gate.T, w_up.T, bg, bu, gg[-1]
    ).T

    sum_a, sum_b = over_z(*ua), over_z(*ub)
    mine = l == h
    sent = swap(jnp.where(mine, sum_b, sum_a).astype(bf16), "l")
    up = jnp.where(mine, sum_a, sum_b) + sent.astype(f32)
    gate = over_z(*gg)

    rows = 2 * d
    first = (2 * z + l) * rows
    news = []
    for w, total in ((w_gate, gate), (w_up, up)):
        held = lax.dynamic_slice_in_dim(w, first, rows, 0).astype(f32)
        near, far = total[:, :q], swap(total[:, q:].astype(bf16), "c").astype(f32)
        both_rows = jnp.where(c == 0, jnp.concatenate([near, far]), jnp.concatenate([far, near]))
        news.append((held + both_rows).astype(bf16))
    return hidden, news[0], news[1]


def solution(mesh):
    fine = Mesh(mesh.devices.reshape(4, 2, 4, 2, 2), AXES)
    pop, mp = ("z", "l"), ("x", "h", "c")
    return jax.shard_map(
        local,
        mesh=fine,
        in_specs=(
            P(pop, mp),
            P(None, mp),
            P(None, mp),
            P(pop, None, mp),
            P(pop, None, mp),
            P(pop, None, mp),
            P(pop, None, mp),
            P(pop),
        ),
        out_specs=(P(pop, mp), P(pop, mp), P(pop, mp)),
        check_vma=False,
    )
```

time: 595 us -> 290 us (0.49)
  waiting for transfers between devices: 411 us -> 105 us
  Pallas kernels: 0 us -> 77.3 us
  starting transfers between devices: 0.2 us -> 73.2 us
  blocking collectives: 69.8 us -> 0 us
  matrix products: 61.2 us -> 0 us
  between operations: 13.9 us -> 1.02 us
  local copies, waits for them, and re-layouts: 31 us -> 18.8 us
  other arithmetic: 7.45 us -> 14.5 us
    reduce_scatter x2 -> x0, waiting for transfers between devices: 283 us -> none  [the longest x1 184 us: local(): lax.psum_scatter(update_maker(full_u, b_up, step_coeff, row_count * lax.a...]
    all_gather x3 -> x0, waiting for transfers between devices: 126 us -> none  [the longest x1 72.1 us: local(): lax.all_gather(weighted_gate, 'mp', axis=2, tiled=True)]
    ppermute x0 -> x37, waiting for transfers between devices: none -> 105 us  [the longest x35 105 us: swap(): return lax.ppermute(v, axis, [(i, (i + shift) % n) for i in range(n)])]
    pallas_call x0 -> x11, Pallas kernels: none -> 77.3 us  [the longest x3 51.4 us: update(): _call(functools.partial(_update_kernel, coeff, slabs, len(seconds), len(a...]
    ppermute x0 -> x37, starting transfers between devices: none -> 73.2 us  [the longest x35 66.9 us: swap(): return lax.ppermute(v, axis, [(i, (i + shift) % n) for i in range(n)])]
    psum x1 -> x0, blocking collectives: 69.8 us -> none  [local(): probe_g, probe_u = lax.psum((part_gate, part_upper), 'mp')]
    dot_general x8 -> x0, matrix products: 61.2 us -> none  [the longest x2 30.1 us: update_maker(): lax.dot_general(left_side, right_side, (((0,), (0,)), ((), ())), preferre...]
    mul x4 -> x0, local copies, waits for them, and re-layouts: 10.8 us -> none  [perturbed(): return base_part + noise_scale * lowrank_noise.reshape(base_part.shape)]
  transfers between devices with their start and end apart: 5 -> 37, of which waited for: 4 -> 10; matrix products, arithmetic and copies ran while one was open for 16% -> 8% of each run, Pallas kernels for 0% -> 27%
where the time goes in v2:
time: 290 us
  waiting for transfers between devices  105 us (36%)
  Pallas kernels  77.3 us (27%)
  starting transfers between devices  73.2 us (25%)
  local copies, waits for them, and re-layouts  18.8 us (6%)
  other arithmetic  14.5 us (5%)
    ppermute x35, waiting for transfers between devices, swap(): return lax.ppermute(v, axis, [(i, (i + shift) % n) for i in range(n)])  105 us
    ppermute x35, starting transfers between devices, swap(): return lax.ppermute(v, axis, [(i, (i + shift) % n) for i in range(n)])  66.9 us
    pallas_call x3, Pallas kernels, update(): _call(functools.partial(_update_kernel, coeff, slabs, len(seconds), len(a...  51.4 us
    pallas_call x1, Pallas kernels, hidden_of(): _call(_hidden_kernel, 'hidden', flops=4 * q * t * (d + rank * m), moved=2...  17.6 us
    unnamed x67, local copies, waits for them, and re-layouts  13.6 us
    ppermute x2, starting transfers between devices, local(): lax.ppermute(sg, ('l', 'h'), [(at_y[i], at_y[j]) for i, j in pairs])  6.31 us
  transfers between devices with their start and end apart: 37, of which 10 were waited for; matrix products, arithmetic and copies ran while one was open for 8% of the time, Pallas kernels for 27%

profile of v2, /device:TPU:1, one launch (start us, length us, event | category | flops | bytes accessed | tf_op | source)
XLA Modules:
  0.0 289.7 jit_solution(3450279846379062250)
XLA Ops:
  0.6 1.5 collective-permute-start.21
  2.1 3.1 %pack.1 = (bf16[896,256]{1,0:T(8,128)(2,1)}, bf16[896,256]{1,0:T(8,128)(2,1)}, bf16[480,256]{1,0:T(8,128)(2,1)}) custom-call(bf16[224,512]{1,0:T(8,128)(2,1)} %bitcast.29, bf16[4,224,256]{2,1,0:T(8,128)(2,1)} %bitcast.27, bf16[4,224,256]{2,1,0:T(8,128)(2,1)} %bitcast.28, f32[1,256]{1,0:T(1,128)} %bitcast.30), custom_call_target="tpu_custom_call" | custom-call | flops 469762048 | bytes 1835008 | tf_op jit(solution)/shard_map/pack/pallas_call | solution.py:88
  5.2 1.3 collective-permute-start.4
  6.5 2.5 collective-permute-start.5
  9.0 1.1 collective-permute-start.6
  10.1 2.9 %collective-permute-start.3 = (bf16[896,256]{1,0:T(8,128)(2,1)}, bf16[896,256]{1,0:T(8,128)(2,1)S(1)}, u32[]{:S(2)}, u32[]{:S(2)}) collective-permute-start(bf16[896,256]{1,0:T(8,128)(2,1)} %get-tuple-element.25.refs_0_), channel_id=1, source_target_pairs={{0,2},{2,0},{1,3},{3,1},{4,6},{6,4},{5,7},{7,5},{8,10},{10,8},{9,1... | collective-permute-start | bytes 1376264 | tf_op jit(solution)/shard_map/ppermute | solution.py:41
  13.0 5.7 %collective-permute-done.4.refs_1_ = bf16[896,256]{1,0:T(8,128)(2,1)S(1)} collective-permute-done((bf16[896,256]{1,0:T(8,128)(2,1)}, bf16[896,256]{1,0:T(8,128)(2,1)S(1)}, u32[]{:S(2)}, u32[]{:S(2)}) %collective-permute-start.4) | collective-permute-done | bytes 458784 | tf_op jit(solution)/shard_map/ppermute | solution.py:41
  18.8 4.9 %collective-permute-start.1 = (bf16[896,256]{1,0:T(8,128)(2,1)}, bf16[896,256]{1,0:T(8,128)(2,1)}, u32[]{:S(2)}, u32[]{:S(2)}) collective-permute-start(bf16[896,256]{1,0:T(8,128)(2,1)} %get-tuple-element.24.s_ref), channel_id=1, source_target_pairs={{16,0},{2,16},{0,2},{17,1},{3,17},{1,3},{20,4},{6,20},{4,6},{21,5}... | collective-permute-start | bytes 1376264 | tf_op jit(solution)/shard_map/ppermute | solution.py:315
  23.7 6.0 %collective-permute-done.5.refs_2_ = bf16[896,256]{1,0:T(8,128)(2,1)S(1)} collective-permute-done((bf16[896,256]{1,0:T(8,128)(2,1)}, bf16[896,256]{1,0:T(8,128)(2,1)S(1)}, u32[]{:S(2)}, u32[]{:S(2)}) %collective-permute-start.5) | collective-permute-done | bytes 458784 | tf_op jit(solution)/shard_map/ppermute | solution.py:41
  29.7 1.4 collective-permute-start.2
  31.1 0.8 copy-done.23
  31.9 0.8 copy-done.24
  32.7 2.0 collective-permute-start.8
  34.7 0.8 collective-permute-start.9
  35.5 1.5 copy.23.refs_0_
  37.0 2.3 pick.1.refs_0_.refs_1_
  39.3 8.9 %collective-permute-start.19 = (bf16[4,1184,256]{2,1,0:T(8,128)(2,1)}, bf16[4,1184,256]{2,1,0:T(8,128)(2,1)}, u32[]{:S(2)}, u32[]{:S(2)}) collective-permute-start(bf16[4,1184,256]{2,1,0:T(8,128)(2,1)} %tie.7), channel_id=1, source_target_pairs={{0,16},{16,0},{1,17},{17,1},{2,18},{18,2},{3,19},{19,3},{4,20},{20... | collective-permute-start | bytes 7274504 | tf_op jit(solution)/shard_map/ppermute | solution.py:41
  48.8 10.4 %collective-permute-start = (bf16[480,256]{1,0:T(8,128)(2,1)S(1)}, bf16[480,256]{1,0:T(8,128)(2,1)S(1)}, u32[]{:S(2)}, u32[]{:S(2)}) collective-permute-start(bf16[480,256]{1,0:T(8,128)(2,1)S(1)} %copy-done.25), channel_id=1, source_target_pairs={{0,2},{2,0},{1,3},{3,1},{4,6},{6,4},{5,7},{7,5},{8,10},{10,8},{9,1... | collective-permute-start | bytes 737288 | tf_op jit(solution)/shard_map/ppermute | solution.py:41
  59.2 0.8 copy-done.20
  60.4 2.3 collective-permute-start.12
  62.7 14.2 %update.3 = (bf16[224,2368]{1,0:T(8,128)(2,1)}, bf16[224,2368]{1,0:T(8,128)(2,1)}, bf16[112,2368]{1,0:T(8,128)(2,1)}, bf16[112,2368]{1,0:T(8,128)(2,1)}, bf16[224,2368]{1,0:T(8,128)(2,1)}) custom-call(s32[4]{0:T(128)} %and_select_fusion.block_ref, bf16[896,256]{1,0:T(8,128)(2,1)} %get-tuple-element.25.refs_0_, bf16[896,256]{1,0:T(8,128)(2,1)} %copy-done.21, ...), custom_call_target="tpu_custom_call" | custom-call | flops 4345298944 | bytes 10928128 | tf_op jit(solution)/shard_map/update/pallas_call | solution.py:187
  77.0 28.9 %collective-permute-done = bf16[480,256]{1,0:T(8,128)(2,1)S(1)} collective-permute-done((bf16[480,256]{1,0:T(8,128)(2,1)S(1)}, bf16[480,256]{1,0:T(8,128)(2,1)S(1)}, u32[]{:S(2)}, u32[]{:S(2)}) %collective-permute-start) | collective-permute-done | bytes 245792 | tf_op jit(solution)/shard_map/ppermute | solution.py:41
  106.6 1.6 collective-permute-start.28
  108.2 2.0 constant_dynamic-slice_fusion
  110.2 1.6 copy.19
  111.7 1.8 pad_maximum_fusion.3.refs_0_
  113.5 2.9 %collective-permute-start.18 = (bf16[4,1184,256]{2,1,0:T(8,128)(2,1)}, bf16[4,1184,256]{2,1,0:T(8,128)(2,1)}, u32[]{:S(2)}, u32[]{:S(2)}) collective-permute-start(bf16[4,1184,256]{2,1,0:T(8,128)(2,1)} %bitcast.15), channel_id=1, source_target_pairs={{0,1},{1,0},{2,3},{3,2},{4,5},{5,4},{6,7},{7,6},{8,9},{9,8},{10,11... | collective-permute-start | bytes 7274504 | tf_op jit(solution)/shard_map/ppermute | solution.py:41
  116.5 0.7 collective-permute-start.13
  117.2 1.9 collective-permute-start.27
  119.2 14.2 %update.4 = (bf16[224,2368]{1,0:T(8,128)(2,1)}, bf16[224,2368]{1,0:T(8,128)(2,1)}, bf16[112,2368]{1,0:T(8,128)(2,1)}, bf16[112,2368]{1,0:T(8,128)(2,1)}, bf16[224,2368]{1,0:T(8,128)(2,1)}) custom-call(s32[4]{0:T(128)} %and_select_fusion.block_ref, bf16[896,256]{1,0:T(8,128)(2,1)} %tie.4.refs_0_, bf16[896,256]{1,0:T(8,128)(2,1)} %copy-done.19, ...), custom_call_target="tpu_custom_call" | custom-call | flops 4345298944 | bytes 10928128 | tf_op jit(solution)/shard_map/update/pallas_call | solution.py:187
  133.4 1.5 convert_element_type.85
  135.0 1.8 collective-permute-start.31
  137.0 5.3 %collective-permute-done.27 = bf16[224,2368]{1,0:T(8,128)(2,1)S(1)} collective-permute-done((bf16[224,2368]{1,0:T(8,128)(2,1)}, bf16[224,2368]{1,0:T(8,128)(2,1)S(1)}, u32[]{:S(2)}, u32[]{:S(2)}) %collective-permute-start.27) | collective-permute-done | bytes 1060896 | tf_op jit(solution)/shard_map/ppermute | solution.py:41
  142.3 3.1 %collective-permute-start.20 = (bf16[4,1184,256]{2,1,0:T(8,128)(2,1)}, bf16[4,1184,256]{2,1,0:T(8,128)(2,1)}, u32[]{:S(2)}, u32[]{:S(2)}) collective-permute-start(bf16[4,1184,256]{2,1,0:T(8,128)(2,1)} %collective-permute-done.19.refs_6_), channel_id=1, source_target_pairs={{0,1},{1,0},{2,3},{3,2},{4,5},{5,4},{6,7},{7,6},{8,9},{9,8},{10,11... | collective-permute-start | bytes 7274504 | tf_op jit(solution)/shard_map/ppermute | solution.py:41
  145.5 20.1 %collective-permute-done.31 = bf16[224,2368]{1,0:T(8,128)(2,1)S(1)} collective-permute-done((bf16[224,2368]{1,0:T(8,128)(2,1)S(1)}, bf16[224,2368]{1,0:T(8,128)(2,1)S(1)}, u32[]{:S(2)}, u32[]{:S(2)}) %collective-permute-start.31) | collective-permute-done | bytes 1060896 | tf_op jit(solution)/shard_map/ppermute | solution.py:41
  165.6 1.3 collective-permute-start.29
  167.0 1.5 collective-permute-start.30
  168.6 10.4 %collective-permute-done.29 = bf16[112,2368]{1,0:T(8,128)(2,1)S(1)} collective-permute-done((bf16[112,2368]{1,0:T(8,128)(2,1)S(1)}, bf16[112,2368]{1,0:T(8,128)(2,1)S(1)}, u32[]{:S(2)}, u32[]{:S(2)}) %collective-permute-start.29) | collective-permute-done | bytes 530464 | tf_op jit(solution)/shard_map/ppermute | solution.py:41
  179.0 1.2 collective-permute-start.34
  180.8 9.3 %collective-permute-done.34 = bf16[112,2368]{1,0:T(8,128)(2,1)S(1)} collective-permute-done((bf16[112,2368]{1,0:T(8,128)(2,1)S(1)}, bf16[112,2368]{1,0:T(8,128)(2,1)S(1)}, u32[]{:S(2)}, u32[]{:S(2)}) %collective-permute-start.34) | collective-permute-done | bytes 530464 | tf_op jit(solution)/shard_map/ppermute | solution.py:41
  190.2 2.4 collective-permute-start.14
  192.6 1.5 collective-permute-start.15
  194.5 1.4 select_convert_fusion
  195.9 0.8 collective-permute-start.35
  196.6 22.9 %update.5 = (bf16[224,2368]{1,0:T(8,128)(2,1)}, bf16[224,2368]{1,0:T(8,128)(2,1)}, bf16[112,2368]{1,0:T(8,128)(2,1)}, bf16[112,2368]{1,0:T(8,128)(2,1)}, bf16[224,2368]{1,0:T(8,128)(2,1)}) custom-call(s32[4]{0:T(128)} %and_select_fusion.block_ref, bf16[1792,256]{1,0:T(8,128)(2,1)} %tie.5.refs_0_, bf16[1792,256]{1,0:T(8,128)(2,1)} %copy-done.12, ...), custom_call_target="tpu_custom_call" | custom-call | flops 8690597888 | bytes 17612800 | tf_op jit(solution)/shard_map/update/pallas_call | solution.py:187
  219.6 2.2 collective-permute-start.22
  221.7 3.0 %constant_dynamic-slice_fusion.1 = bf16[448,1184]{0,1:T(8,128)(2,1)} fusion(bf16[3584,1184]{0,1:T(8,128)(2,1)} %param.10, s32[]{:T(128)S(6)} %select_n.36), kind=kLoop, calls=%fused_computation.41 | loop fusion | bytes 2121732 | tf_op jit(solution)/shard_map/dynamic_slice | solution.py:342
  224.7 2.4 copy.18
  227.7 2.9 %tokens.1 = (bf16[4,2,224,512]{3,2,1,0:T(8,128)(2,1)}, f32[8,512]{1,0:T(8,128)}) custom-call(s32[2]{0:T(128)} %pad_add_fusion.at_ref, bf16[2,480,256]{2,1,0:T(8,128)(2,1)} %tie.6.refs_0_, bf16[2,480,256]{2,1,0:T(8,128)(2,1)} %collective-permute-done.13.refs_1_, bf16[2,480,256]{2,1,0:T(8,128)(2,1)} %collective-permute-done.14.refs_2_, ...), custom_call_target="tpu_custom_call" | custom-call | bytes 3932160 | tf_op jit(solution)/shard_map/tokens/pallas_call | solution.py:234
  230.6 4.8 %collective-permute-start.16 = (bf16[4,2,224,512]{3,2,1,0:T(8,128)(2,1)}, bf16[4,2,224,512]{3,2,1,0:T(8,128)(2,1)}, u32[]{:S(2)}, u32[]{:S(2)}) collective-permute-start(bf16[4,2,224,512]{3,2,1,0:T(8,128)(2,1)} %get-tuple-element.26.mine_ref), channel_id=1, source_target_pairs={{0,1},{1,0},{2,3},{3,2},{4,5},{5,4},{6,7},{7,6},{8,9},{9,8},{10,11... | collective-permute-start | bytes 5505032 | tf_op jit(solution)/shard_map/ppermute | solution.py:41
  235.4 1.6 convert_add_fusion
  237.3 1.1 copy-done.2
  239.2 2.4 collective-permute-done.22
  241.6 1.1 slice_add_fusion.10
  242.8 2.7 collective-permute-start.25
  245.5 16.5 %collective-permute-done.23 = bf16[224,2368]{1,0:T(8,128)(2,1)S(1)} collective-permute-done((bf16[224,2368]{1,0:T(8,128)(2,1)}, bf16[224,2368]{1,0:T(8,128)(2,1)S(1)}, u32[]{:S(2)}, u32[]{:S(2)}) %collective-permute-start.23) | collective-permute-done | bytes 1060896 | tf_op jit(solution)/shard_map/ppermute | solution.py:41
  261.9 1.0 copy-done.10
  263.7 17.6 %hidden.1 = bf16[1184,512]{1,0:T(8,128)(2,1)} custom-call(s32[1]{0:T(128)} %bitcast.c_ref, bf16[4,2,224,512]{3,2,1,0:T(8,128)(2,1)} %get-tuple-element.26.mine_ref, bf16[4,2,224,512]{3,2,1,0:T(8,128)(2,1)} %collective-permute-done.16.other_ref, f32[8,512]{1,0:T(8,128)} %get-tuple-element.27.p0_ref, f32[8,512]{1,0:T(8,128)} %copy-done.30, ...), custom_call_target="tpu_custom_call" | custom-call | flops 11173625856 | bytes 26705920 | tf_op jit(solution)/shard_map/hidden/pallas_call | solution.py:282
  281.4 1.1 copy-done.11
  282.6 1.4 fusion.11
  284.2 1.4 collective-permute-start.26
  285.7 1.4 fusion.3
  287.4 1.0 copy-done.4
  288.4 1.4 fusion.1
  (116 shorter events, 6.4 us)
Async XLA Ops:
  0.6 59.8 %collective-permute-start.21 = (bf16[4,1184,256]{2,1,0:T(8,128)(2,1)}, bf16[4,1184,256]{2,1,0:T(8,128)(2,1)}, u32[]{:S(2)}, u32[]{:S(2)}) collective-permute-start(bf16[4,1184,256]{2,1,0:T(8,128)(2,1)} %bitcast.23), channel_id=1, source_target_pairs={{0,1},{1,0},{2,3},{3,2},{4,5},{5,4},{6,7},{7,6},{8,9},{9,8},{10,11... | collective-permute-start | bytes 7274504 | tf_op jit(solution)/shard_map/ppermute | solution.py:41
  2.1 33.3 %copy-start.5 = (bf16[256,4,1184]{0,2,1:T(8,128)(2,1)S(1)}, bf16[256,4,1184]{0,2,1:T(8,128)(2,1)}, u32[]{:S(2)}) copy-start(bf16[256,4,1184]{0,2,1:T(8,128)(2,1)} %param.14) | copy-start | bytes 7274500
  5.2 13.6 %collective-permute-start.4 = (bf16[896,256]{1,0:T(8,128)(2,1)}, bf16[896,256]{1,0:T(8,128)(2,1)S(1)}, u32[]{:S(2)}, u32[]{:S(2)}) collective-permute-start(bf16[896,256]{1,0:T(8,128)(2,1)} %get-tuple-element.25.refs_0_), channel_id=1, source_target_pairs={{0,4},{4,8},{8,12},{12,0},{1,5},{5,9},{9,13},{13,1},{2,6},{6,10},{... | collective-permute-start | bytes 1376264 | tf_op jit(solution)/shard_map/ppermute | solution.py:41
  6.5 23.1 %collective-permute-start.5 = (bf16[896,256]{1,0:T(8,128)(2,1)}, bf16[896,256]{1,0:T(8,128)(2,1)S(1)}, u32[]{:S(2)}, u32[]{:S(2)}) collective-permute-start(bf16[896,256]{1,0:T(8,128)(2,1)} %get-tuple-element.25.refs_0_), channel_id=1, source_target_pairs={{0,8},{4,12},{8,0},{12,4},{1,9},{5,13},{9,1},{13,5},{2,10},{6,14},... | collective-permute-start | bytes 1376264 | tf_op jit(solution)/shard_map/ppermute | solution.py:41
  9.0 22.1 %collective-permute-start.6 = (bf16[896,256]{1,0:T(8,128)(2,1)}, bf16[896,256]{1,0:T(8,128)(2,1)S(1)}, u32[]{:S(2)}, u32[]{:S(2)}) collective-permute-start(bf16[896,256]{1,0:T(8,128)(2,1)} %get-tuple-element.25.refs_0_), channel_id=1, source_target_pairs={{0,12},{4,0},{8,4},{12,8},{1,13},{5,1},{9,5},{13,9},{2,14},{6,2},{... | collective-permute-start | bytes 1376264 | tf_op jit(solution)/shard_map/ppermute | solution.py:41
  10.1 21.0 %collective-permute-start.3 = (bf16[896,256]{1,0:T(8,128)(2,1)}, bf16[896,256]{1,0:T(8,128)(2,1)S(1)}, u32[]{:S(2)}, u32[]{:S(2)}) collective-permute-start(bf16[896,256]{1,0:T(8,128)(2,1)} %get-tuple-element.25.refs_0_), channel_id=1, source_target_pairs={{0,2},{2,0},{1,3},{3,1},{4,6},{6,4},{5,7},{7,5},{8,10},{10,8},{9,1... | collective-permute-start | bytes 1376264 | tf_op jit(solution)/shard_map/ppermute | solution.py:41
  18.8 12.3 %copy-start.21 = (bf16[896,256]{1,0:T(8,128)(2,1)}, bf16[896,256]{1,0:T(8,128)(2,1)S(1)}, u32[]{:S(2)}) copy-start(bf16[896,256]{1,0:T(8,128)(2,1)S(1)} %collective-permute-done.4.refs_1_) | copy-start | bytes 1376260
  18.8 15.9 %collective-permute-start.1 = (bf16[896,256]{1,0:T(8,128)(2,1)}, bf16[896,256]{1,0:T(8,128)(2,1)}, u32[]{:S(2)}, u32[]{:S(2)}) collective-permute-start(bf16[896,256]{1,0:T(8,128)(2,1)} %get-tuple-element.24.s_ref), channel_id=1, source_target_pairs={{16,0},{2,16},{0,2},{17,1},{3,17},{1,3},{20,4},{6,20},{4,6},{21,5}... | collective-permute-start | bytes 1376264 | tf_op jit(solution)/shard_map/ppermute | solution.py:315
  29.7 1.4 copy-start.22
  29.7 7.3 %collective-permute-start.2 = (bf16[896,256]{1,0:T(8,128)(2,1)}, bf16[896,256]{1,0:T(8,128)(2,1)}, u32[]{:S(2)}, u32[]{:S(2)}) collective-permute-start(bf16[896,256]{1,0:T(8,128)(2,1)} %get-tuple-element.24.s_ref), channel_id=1, source_target_pairs={{18,16},{16,2},{2,18},{19,17},{17,3},{3,19},{22,20},{20,6},{6,22},... | collective-permute-start | bytes 1376264 | tf_op jit(solution)/shard_map/ppermute | solution.py:315
  32.7 16.1 %collective-permute-start.7 = (bf16[896,256]{1,0:T(8,128)(2,1)}, bf16[896,256]{1,0:T(8,128)(2,1)S(1)}, u32[]{:S(2)}, u32[]{:S(2)}) collective-permute-start(bf16[896,256]{1,0:T(8,128)(2,1)} %tie.4.refs_0_), channel_id=1, source_target_pairs={{0,4},{4,8},{8,12},{12,0},{1,5},{5,9},{9,13},{13,1},{2,6},{6,10},{... | collective-permute-start | bytes 1376264 | tf_op jit(solution)/shard_map/ppermute | solution.py:41
  32.7 26.6 %collective-permute-start.8 = (bf16[896,256]{1,0:T(8,128)(2,1)}, bf16[896,256]{1,0:T(8,128)(2,1)S(1)}, u32[]{:S(2)}, u32[]{:S(2)}) collective-permute-start(bf16[896,256]{1,0:T(8,128)(2,1)} %tie.4.refs_0_), channel_id=1, source_target_pairs={{0,8},{4,12},{8,0},{12,4},{1,9},{5,13},{9,1},{13,5},{2,10},{6,14},... | collective-permute-start | bytes 1376264 | tf_op jit(solution)/shard_map/ppermute | solution.py:41
  34.7 24.6 %collective-permute-start.9 = (bf16[896,256]{1,0:T(8,128)(2,1)}, bf16[896,256]{1,0:T(8,128)(2,1)}, u32[]{:S(2)}, u32[]{:S(2)}) collective-permute-start(bf16[896,256]{1,0:T(8,128)(2,1)} %tie.4.refs_0_), channel_id=1, source_target_pairs={{0,12},{4,0},{8,4},{12,8},{1,13},{5,1},{9,5},{13,9},{2,14},{6,2},{... | collective-permute-start | bytes 1376264 | tf_op jit(solution)/shard_map/ppermute | solution.py:41
  39.3 8.9 %copy-start.31 = (s32[4]{0:T(128)S(1)}, s32[4]{0:T(128)}, u32[]{:S(2)}) copy-start(s32[4]{0:T(128)} %constant.44) | copy-start | bytes 52
  39.3 9.5 %copy-start.25 = (bf16[480,256]{1,0:T(8,128)(2,1)S(1)}, bf16[480,256]{1,0:T(8,128)(2,1)}, u32[]{:S(2)}) copy-start(bf16[480,256]{1,0:T(8,128)(2,1)} %get-tuple-element.23) | copy-start | bytes 737284
  39.3 97.6 %collective-permute-start.19 = (bf16[4,1184,256]{2,1,0:T(8,128)(2,1)}, bf16[4,1184,256]{2,1,0:T(8,128)(2,1)}, u32[]{:S(2)}, u32[]{:S(2)}) collective-permute-start(bf16[4,1184,256]{2,1,0:T(8,128)(2,1)} %tie.7), channel_id=1, source_target_pairs={{0,16},{16,0},{1,17},{17,1},{2,18},{18,2},{3,19},{19,3},{4,20},{20... | collective-permute-start | bytes 7274504 | tf_op jit(solution)/shard_map/ppermute | solution.py:41
  48.8 10.4 %copy-start.19 = (bf16[896,256]{1,0:T(8,128)(2,1)}, bf16[896,256]{1,0:T(8,128)(2,1)S(1)}, u32[]{:S(2)}) copy-start(bf16[896,256]{1,0:T(8,128)(2,1)S(1)} %collective-permute-done.7.refs_1_) | copy-start | bytes 1376260
  48.8 57.1 %collective-permute-start = (bf16[480,256]{1,0:T(8,128)(2,1)S(1)}, bf16[480,256]{1,0:T(8,128)(2,1)S(1)}, u32[]{:S(2)}, u32[]{:S(2)}) collective-permute-start(bf16[480,256]{1,0:T(8,128)(2,1)S(1)} %copy-done.25), channel_id=1, source_target_pairs={{0,2},{2,0},{1,3},{3,1},{4,6},{6,4},{5,7},{7,5},{8,10},{10,8},{9,1... | collective-permute-start | bytes 737288 | tf_op jit(solution)/shard_map/ppermute | solution.py:41
  60.0 53.5 %collective-permute-start.10 = (bf16[1792,256]{1,0:T(8,128)(2,1)}, bf16[1792,256]{1,0:T(8,128)(2,1)S(1)}, u32[]{:S(2)}, u32[]{:S(2)}) collective-permute-start(bf16[1792,256]{1,0:T(8,128)(2,1)} %tie.5.refs_0_), channel_id=1, source_target_pairs={{0,4},{4,8},{8,12},{12,0},{1,5},{5,9},{9,13},{13,1},{2,6},{6,10},{... | collective-permute-start | bytes 2752520 | tf_op jit(solution)/shard_map/ppermute | solution.py:41
  60.0 56.4 %collective-permute-start.11 = (bf16[1792,256]{1,0:T(8,128)(2,1)}, bf16[1792,256]{1,0:T(8,128)(2,1)}, u32[]{:S(2)}, u32[]{:S(2)}) collective-permute-start(bf16[1792,256]{1,0:T(8,128)(2,1)} %tie.5.refs_0_), channel_id=1, source_target_pairs={{0,8},{4,12},{8,0},{12,4},{1,9},{5,13},{9,1},{13,5},{2,10},{6,14},... | collective-permute-start | bytes 2752520 | tf_op jit(solution)/shard_map/ppermute | solution.py:41
  60.4 56.0 %collective-permute-start.12 = (bf16[1792,256]{1,0:T(8,128)(2,1)}, bf16[1792,256]{1,0:T(8,128)(2,1)}, u32[]{:S(2)}, u32[]{:S(2)}) collective-permute-start(bf16[1792,256]{1,0:T(8,128)(2,1)} %tie.5.refs_0_), channel_id=1, source_target_pairs={{0,12},{4,0},{8,4},{12,8},{1,13},{5,1},{9,5},{13,9},{2,14},{6,2},{... | collective-permute-start | bytes 2752520 | tf_op jit(solution)/shard_map/ppermute | solution.py:41
  106.6 28.4 %collective-permute-start.28 = (bf16[224,2368]{1,0:T(8,128)(2,1)}, bf16[224,2368]{1,0:T(8,128)(2,1)S(1)}, u32[]{:S(2)}, u32[]{:S(2)}) collective-permute-start(bf16[224,2368]{1,0:T(8,128)(2,1)} %get-tuple-element.37), channel_id=1, source_target_pairs={{0,32},{32,64},{64,96},{96,0},{1,33},{33,65},{65,97},{97,1},{2,34}... | collective-permute-start | bytes 3182600 | tf_op jit(solution)/shard_map/ppermute | solution.py:41
  110.2 1.6 copy-start.26
  113.5 5.5 %copy-start.7 = (bf16[224,2368]{1,0:T(8,128)(2,1)S(1)}, bf16[224,2368]{1,0:T(8,128)(2,1)}, u32[]{:S(2)}) copy-start(bf16[224,2368]{1,0:T(8,128)(2,1)} %get-tuple-element.28.refs_6_) | copy-start | bytes 3182596
  113.5 2.9 %copy-start.12 = (bf16[1792,256]{1,0:T(8,128)(2,1)}, bf16[1792,256]{1,0:T(8,128)(2,1)S(1)}, u32[]{:S(2)}) copy-start(bf16[1792,256]{1,0:T(8,128)(2,1)S(1)} %collective-permute-done.10.refs_1_) | copy-start | bytes 2752516
  113.5 82.3 %collective-permute-start.18 = (bf16[4,1184,256]{2,1,0:T(8,128)(2,1)}, bf16[4,1184,256]{2,1,0:T(8,128)(2,1)}, u32[]{:S(2)}, u32[]{:S(2)}) collective-permute-start(bf16[4,1184,256]{2,1,0:T(8,128)(2,1)} %bitcast.15), channel_id=1, source_target_pairs={{0,1},{1,0},{2,3},{3,2},{4,5},{5,4},{6,7},{7,6},{8,9},{9,8},{10,11... | collective-permute-start | bytes 7274504 | tf_op jit(solution)/shard_map/ppermute | solution.py:41
  116.5 111.3 %collective-permute-start.13 = (bf16[2,480,256]{2,1,0:T(8,128)(2,1)}, bf16[2,480,256]{2,1,0:T(8,128)(2,1)}, u32[]{:S(2)}, u32[]{:S(2)}) collective-permute-start(bf16[2,480,256]{2,1,0:T(8,128)(2,1)} %tie.6.refs_0_), channel_id=1, source_target_pairs={{0,4},{4,8},{8,12},{12,0},{1,5},{5,9},{9,13},{13,1},{2,6},{6,10},{... | collective-permute-start | bytes 1474568 | tf_op jit(solution)/shard_map/ppermute | solution.py:41
  117.2 25.1 %collective-permute-start.27 = (bf16[224,2368]{1,0:T(8,128)(2,1)}, bf16[224,2368]{1,0:T(8,128)(2,1)S(1)}, u32[]{:S(2)}, u32[]{:S(2)}) collective-permute-start(bf16[224,2368]{1,0:T(8,128)(2,1)} %get-tuple-element.35), channel_id=1, source_target_pairs={{0,96},{32,0},{64,32},{96,64},{1,97},{33,1},{65,33},{97,65},{2,98}... | collective-permute-start | bytes 3182600 | tf_op jit(solution)/shard_map/ppermute | solution.py:41
  133.4 1.6 copy-start.29
  133.4 3.4 %copy-start.14 = (bf16[112,2368]{1,0:T(8,128)(2,1)S(1)}, bf16[112,2368]{1,0:T(8,128)(2,1)}, u32[]{:S(2)}) copy-start(bf16[112,2368]{1,0:T(8,128)(2,1)} %get-tuple-element.36) | copy-start | bytes 1591300
  134.9 2.0 copy-start.28
  134.9 10.5 %copy-start.13 = (bf16[112,2368]{1,0:T(8,128)(2,1)S(1)}, bf16[112,2368]{1,0:T(8,128)(2,1)}, u32[]{:S(2)}) copy-start(bf16[112,2368]{1,0:T(8,128)(2,1)} %get-tuple-element.38) | copy-start | bytes 1591300
  135.0 30.6 %collective-permute-start.31 = (bf16[224,2368]{1,0:T(8,128)(2,1)S(1)}, bf16[224,2368]{1,0:T(8,128)(2,1)S(1)}, u32[]{:S(2)}, u32[]{:S(2)}) collective-permute-start(bf16[224,2368]{1,0:T(8,128)(2,1)S(1)} %copy-done.29), channel_id=1, source_target_pairs={{0,96},{32,0},{64,32},{96,64},{1,97},{33,1},{65,33},{97,65},{2,98}... | collective-permute-start | bytes 3182600 | tf_op jit(solution)/shard_map/ppermute | solution.py:41
  136.9 30.0 %copy-start.18 = (bf16[112,2368]{1,0:T(8,128)(2,1)S(1)}, bf16[112,2368]{1,0:T(8,128)(2,1)}, u32[]{:S(2)}) copy-start(bf16[112,2368]{1,0:T(8,128)(2,1)} %get-tuple-element.42) | copy-start | bytes 1591300
  136.9 30.1 %collective-permute-start.32 = (bf16[224,2368]{1,0:T(8,128)(2,1)S(1)}, bf16[224,2368]{1,0:T(8,128)(2,1)S(1)}, u32[]{:S(2)}, u32[]{:S(2)}) collective-permute-start(bf16[224,2368]{1,0:T(8,128)(2,1)S(1)} %copy-done.28), channel_id=1, source_target_pairs={{0,32},{32,64},{64,96},{96,0},{1,33},{33,65},{65,97},{97,1},{2,34}... | collective-permute-start | bytes 3182600 | tf_op jit(solution)/shard_map/ppermute | solution.py:41
  142.3 24.7 %copy-start.8 = (bf16[224,2368]{1,0:T(8,128)(2,1)}, bf16[224,2368]{1,0:T(8,128)(2,1)S(1)}, u32[]{:S(2)}) copy-start(bf16[224,2368]{1,0:T(8,128)(2,1)S(1)} %collective-permute-done.27) | copy-start | bytes 3182596
  142.3 54.3 %collective-permute-start.20 = (bf16[4,1184,256]{2,1,0:T(8,128)(2,1)}, bf16[4,1184,256]{2,1,0:T(8,128)(2,1)}, u32[]{:S(2)}, u32[]{:S(2)}) collective-permute-start(bf16[4,1184,256]{2,1,0:T(8,128)(2,1)} %collective-permute-done.19.refs_6_), channel_id=1, source_target_pairs={{0,1},{1,0},{2,3},{3,2},{4,5},{5,4},{6,7},{7,6},{8,9},{9,8},{10,11... | collective-permute-start | bytes 7274504 | tf_op jit(solution)/shard_map/ppermute | solution.py:41
  145.5 23.0 %copy-start.17 = (bf16[112,2368]{1,0:T(8,128)(2,1)S(1)}, bf16[112,2368]{1,0:T(8,128)(2,1)}, u32[]{:S(2)}) copy-start(bf16[112,2368]{1,0:T(8,128)(2,1)} %get-tuple-element.40) | copy-start | bytes 1591300
  165.6 13.3 %collective-permute-start.29 = (bf16[112,2368]{1,0:T(8,128)(2,1)S(1)}, bf16[112,2368]{1,0:T(8,128)(2,1)S(1)}, u32[]{:S(2)}, u32[]{:S(2)}) collective-permute-start(bf16[112,2368]{1,0:T(8,128)(2,1)S(1)} %slice_add_fusion.9), channel_id=1, source_target_pairs={{0,32},{32,64},{64,96},{96,0},{1,33},{33,65},{65,97},{97,1},{2,34}... | collective-permute-start | bytes 1591304 | tf_op jit(solution)/shard_map/ppermute | solution.py:41
  167.0 13.5 %copy-start.9 = (bf16[224,2368]{1,0:T(8,128)(2,1)S(1)}, bf16[224,2368]{1,0:T(8,128)(2,1)}, u32[]{:S(2)}) copy-start(bf16[224,2368]{1,0:T(8,128)(2,1)} %copy-done.8) | copy-start | bytes 3182596
  167.0 13.2 %collective-permute-start.30 = (bf16[112,2368]{1,0:T(8,128)(2,1)S(1)}, bf16[112,2368]{1,0:T(8,128)(2,1)S(1)}, u32[]{:S(2)}, u32[]{:S(2)}) collective-permute-start(bf16[112,2368]{1,0:T(8,128)(2,1)S(1)} %slice_add_fusion.8), channel_id=1, source_target_pairs={{0,96},{32,0},{64,32},{96,64},{1,97},{33,1},{65,33},{97,65},{2,98}... | collective-permute-start | bytes 1591304 | tf_op jit(solution)/shard_map/ppermute | solution.py:41
  179.0 11.2 %collective-permute-start.34 = (bf16[112,2368]{1,0:T(8,128)(2,1)S(1)}, bf16[112,2368]{1,0:T(8,128)(2,1)S(1)}, u32[]{:S(2)}, u32[]{:S(2)}) collective-permute-start(bf16[112,2368]{1,0:T(8,128)(2,1)S(1)} %slice_add_fusion.6), channel_id=1, source_target_pairs={{0,96},{32,0},{64,32},{96,64},{1,97},{33,1},{65,33},{97,65},{2,98}... | collective-permute-start | bytes 1591304 | tf_op jit(solution)/shard_map/ppermute | solution.py:41
  180.2 12.4 %collective-permute-start.33 = (bf16[112,2368]{1,0:T(8,128)(2,1)S(1)}, bf16[112,2368]{1,0:T(8,128)(2,1)S(1)}, u32[]{:S(2)}, u32[]{:S(2)}) collective-permute-start(bf16[112,2368]{1,0:T(8,128)(2,1)S(1)} %slice_add_fusion.7), channel_id=1, source_target_pairs={{0,32},{32,64},{64,96},{96,0},{1,33},{33,65},{65,97},{97,1},{2,34}... | collective-permute-start | bytes 1591304 | tf_op jit(solution)/shard_map/ppermute | solution.py:41
  190.2 37.6 %collective-permute-start.14 = (bf16[2,480,256]{2,1,0:T(8,128)(2,1)}, bf16[2,480,256]{2,1,0:T(8,128)(2,1)}, u32[]{:S(2)}, u32[]{:S(2)}) collective-permute-start(bf16[2,480,256]{2,1,0:T(8,128)(2,1)} %tie.6.refs_0_), channel_id=1, source_target_pairs={{0,8},{4,12},{8,0},{12,4},{1,9},{5,13},{9,1},{13,5},{2,10},{6,14},... | collective-permute-start | bytes 1474568 | tf_op jit(solution)/shard_map/ppermute | solution.py:41
  192.6 35.2 %collective-permute-start.15 = (bf16[2,480,256]{2,1,0:T(8,128)(2,1)}, bf16[2,480,256]{2,1,0:T(8,128)(2,1)}, u32[]{:S(2)}, u32[]{:S(2)}) collective-permute-start(bf16[2,480,256]{2,1,0:T(8,128)(2,1)} %tie.6.refs_0_), channel_id=1, source_target_pairs={{0,12},{4,0},{8,4},{12,8},{1,13},{5,1},{9,5},{13,9},{2,14},{6,2},{... | collective-permute-start | bytes 1474568 | tf_op jit(solution)/shard_map/ppermute | solution.py:41
  194.5 1.4 copy-start
  195.9 39.6 %collective-permute-start.35 = (bf16[224,2368]{1,0:T(8,128)(2,1)}, bf16[224,2368]{1,0:T(8,128)(2,1)}, u32[]{:S(2)}, u32[]{:S(2)}) collective-permute-start(bf16[224,2368]{1,0:T(8,128)(2,1)} %select_convert_fusion), channel_id=1, source_target_pairs={{0,16},{16,0},{1,17},{17,1},{2,18},{18,2},{3,19},{19,3},{4,20},{20... | collective-permute-start | bytes 3182600 | tf_op jit(solution)/shard_map/ppermute | solution.py:41
  219.6 22.1 %collective-permute-start.22 = (bf16[224,2368]{1,0:T(8,128)(2,1)}, bf16[224,2368]{1,0:T(8,128)(2,1)}, u32[]{:S(2)}, u32[]{:S(2)}) collective-permute-start(bf16[224,2368]{1,0:T(8,128)(2,1)} %get-tuple-element.31), channel_id=1, source_target_pairs={{0,96},{32,0},{64,32},{96,64},{1,97},{33,1},{65,33},{97,65},{2,98}... | collective-permute-start | bytes 3182600 | tf_op jit(solution)/shard_map/ppermute | solution.py:41
  227.1 8.3 %copy-start.1 = (f32[112,2368]{1,0:T(8,128)S(1)}, f32[112,2368]{1,0:T(8,128)}, u32[]{:S(2)}) copy-start(f32[112,2368]{1,0:T(8,128)} %copy-done) | copy-start | bytes 3182596
  230.6 32.5 %collective-permute-start.16 = (bf16[4,2,224,512]{3,2,1,0:T(8,128)(2,1)}, bf16[4,2,224,512]{3,2,1,0:T(8,128)(2,1)}, u32[]{:S(2)}, u32[]{:S(2)}) collective-permute-start(bf16[4,2,224,512]{3,2,1,0:T(8,128)(2,1)} %get-tuple-element.26.mine_ref), channel_id=1, source_target_pairs={{0,1},{1,0},{2,3},{3,2},{4,5},{5,4},{6,7},{7,6},{8,9},{9,8},{10,11... | collective-permute-start | bytes 5505032 | tf_op jit(solution)/shard_map/ppermute | solution.py:41
  235.4 27.7 %collective-permute-start.17 = (f32[8,512]{1,0:T(8,128)}, f32[8,512]{1,0:T(8,128)S(1)}, u32[]{:S(2)}, u32[]{:S(2)}) collective-permute-start(f32[8,512]{1,0:T(8,128)} %get-tuple-element.27.p0_ref), channel_id=1, source_target_pairs={{0,1},{1,0},{2,3},{3,2},{4,5},{5,4},{6,7},{7,6},{8,9},{9,8},{10,11... | collective-permute-start | bytes 49160 | tf_op jit(solution)/shard_map/ppermute | solution.py:41
  235.4 26.5 %collective-permute-start.23 = (bf16[224,2368]{1,0:T(8,128)(2,1)}, bf16[224,2368]{1,0:T(8,128)(2,1)S(1)}, u32[]{:S(2)}, u32[]{:S(2)}) collective-permute-start(bf16[224,2368]{1,0:T(8,128)(2,1)} %get-tuple-element.33), channel_id=1, source_target_pairs={{0,32},{32,64},{64,96},{96,0},{1,33},{33,65},{65,97},{97,1},{2,34}... | collective-permute-start | bytes 3182600 | tf_op jit(solution)/shard_map/ppermute | solution.py:41
  237.0 1.3 copy-start.2
  237.3 1.8 copy-start.6
  238.3 43.0 %collective-permute-start.36 = (bf16[224,1184]{1,0:T(8,128)(2,1)S(1)}, bf16[224,1184]{1,0:T(8,128)(2,1)S(1)}, u32[]{:S(2)}, u32[]{:S(2)}) collective-permute-start(bf16[224,1184]{1,0:T(8,128)(2,1)S(1)} %slice.149), channel_id=1, source_target_pairs={{0,1},{1,0},{2,3},{3,2},{4,5},{5,4},{6,7},{7,6},{8,9},{9,8},{10,11... | collective-permute-start | bytes 1591304 | tf_op jit(solution)/shard_map/ppermute | solution.py:41
  239.0 2.6 copy-start.16
  239.2 23.7 %copy-start.15 = (bf16[112,2368]{1,0:T(8,128)(2,1)S(1)}, bf16[112,2368]{1,0:T(8,128)(2,1)}, u32[]{:S(2)}) copy-start(bf16[112,2368]{1,0:T(8,128)(2,1)} %get-tuple-element.32) | copy-start | bytes 1591300
  242.8 38.6 %collective-permute-start.25 = (bf16[112,2368]{1,0:T(8,128)(2,1)S(1)}, bf16[112,2368]{1,0:T(8,128)(2,1)S(1)}, u32[]{:S(2)}, u32[]{:S(2)}) collective-permute-start(bf16[112,2368]{1,0:T(8,128)(2,1)S(1)} %slice_add_fusion.10), channel_id=1, source_target_pairs={{0,96},{32,0},{64,32},{96,64},{1,97},{33,1},{65,33},{97,65},{2,98}... | collective-permute-start | bytes 1591304 | tf_op jit(solution)/shard_map/ppermute | solution.py:41
  263.0 18.4 %collective-permute-start.24 = (bf16[112,2368]{1,0:T(8,128)(2,1)S(1)}, bf16[112,2368]{1,0:T(8,128)(2,1)S(1)}, u32[]{:S(2)}, u32[]{:S(2)}) collective-permute-start(bf16[112,2368]{1,0:T(8,128)(2,1)S(1)} %slice_add_fusion.11), channel_id=1, source_target_pairs={{0,32},{32,64},{64,96},{96,0},{1,33},{33,65},{65,97},{97,1},{2,34}... | collective-permute-start | bytes 1591304 | tf_op jit(solution)/shard_map/ppermute | solution.py:41
  281.3 1.2 copy-start.11
  284.0 1.7 slice-start
  284.0 1.7 copy-start.3
  284.2 3.0 %collective-permute-start.26 = (bf16[224,1184]{1,0:T(8,128)(2,1)S(1)}, bf16[224,1184]{1,0:T(8,128)(2,1)S(1)}, u32[]{:S(2)}, u32[]{:S(2)}) collective-permute-start(bf16[224,1184]{1,0:T(8,128)(2,1)S(1)} %fusion.5), channel_id=1, source_target_pairs={{0,1},{1,0},{2,3},{3,2},{4,5},{5,4},{6,7},{7,6},{8,9},{9,8},{10,11... | collective-permute-start | bytes 1591304 | tf_op jit(solution)/shard_map/ppermute | solution.py:41
  287.1 1.3 copy-start.4
  (6 other events, 4.7 us)

commit v3 on v2

v3 whole, which is shorter than its diff:
```python
import functools

import jax
import jax.numpy as jnp
from jax import lax
from jax.experimental import pallas as pl
from jax.experimental.pallas import tpu as pltpu
from jax.sharding import Mesh
from jax.sharding import PartitionSpec as P

bf16 = jnp.bfloat16
f32 = jnp.float32
noise_scale = 0.5
AXES = ("z", "l", "x", "h", "c")
RING = 4
VMEM = 58 * 1024 * 1024
HINT = 1
NT = (((1,), (1,)), ((), ()))
TN = (((0,), (0,)), ((), ()))


def _call(kernel, name, flops=0, moved=0, **kw):
    return pl.pallas_call(
        kernel,
        name=name,
        compiler_params=pltpu.CompilerParams(vmem_limit_bytes=VMEM),
        cost_estimate=pl.CostEstimate(flops=flops // HINT, bytes_accessed=moved // HINT, transcendentals=0),
        **kw,
    )


def _any(n):
    return [pl.BlockSpec(memory_space=pl.ANY)] * n


FULL = pl.BlockSpec(memory_space=pltpu.VMEM)
SCALARS = pl.BlockSpec(memory_space=pltpu.SMEM)


def swap(v, axis, shift=1):
    n = lax.axis_size(axis)
    return lax.ppermute(v, axis, [(i, (i + shift) % n) for i in range(n)])


def join(vs, *after):
    n = len(vs)
    return _call(
        lambda *refs: None,
        "join",
        in_specs=_any(n + len(after)),
        out_specs=_any(n),
        out_shape=[jax.ShapeDtypeStruct(v.shape, v.dtype) for v in vs],
        input_output_aliases={i: i for i in range(n)},
    )(*vs, *after)


def tie(v, *after):
    return join([v], *after)[0]


def _own_mask(members, tokens):
    m = lax.broadcasted_iota(jnp.int32, (members, tokens), 0)
    t = lax.broadcasted_iota(jnp.int32, (members, tokens), 1)
    return jnp.logical_or(t == 2 * m, t == 2 * m + 1)


def _pack_kernel(tok_ref, ag_ref, au_ref, fit_ref, sg_ref, su_ref, all_ref):
    rank, d, m = ag_ref.shape
    tok = tok_ref[...]
    t = tok.shape[1]
    fit = fit_ref[...]
    mask = _own_mask(m, t)
    rows = []
    for a_ref, s_refs in ((ag_ref, (sg_ref,)), (au_ref, (su_ref, all_ref))):
        for r in range(rank):
            a = a_ref[r]
            for s_ref in s_refs:
                s_ref[r * d : (r + 1) * d, :] = (a.astype(f32) * fit).astype(bf16)
            s = lax.dot_general(a, tok, TN, preferred_element_type=f32)
            rows.append(jnp.sum(jnp.where(mask, s, 0.0), axis=0, keepdims=True))
    part = jnp.concatenate(rows, axis=0)
    high = part.astype(bf16)
    low = (part - high.astype(f32)).astype(bf16)
    at = rank * d
    for v in (tok, jnp.concatenate([high, low], axis=0)):
        for lo in range(0, t, m):
            all_ref[at : at + v.shape[0], :] = v[:, lo : lo + m]
            at += v.shape[0]


def pack(tok_t, ag, au, fit):
    rank, d, m = ag.shape
    t = tok_t.shape[1]
    pay = (d + 4 * rank) * (t // m)
    return _call(
        _pack_kernel,
        "pack",
        flops=4 * rank * d * m * t,
        moved=8 * rank * d * m,
        in_specs=[FULL] * 4,
        out_specs=[FULL] * 3,
        out_shape=[jax.ShapeDtypeStruct((n, m), bf16) for n in (rank * d, rank * d, rank * d + pay)],
    )(tok_t, ag, au, fit)


def _pick_kernel(y_ref, s_ref, pa_ref, pb_ref, all_ref, *refs):
    out_ref = refs[-1]
    n = s_ref.shape[0]
    y = y_ref[0]
    for where, at, ref in (
        (y == 1, 0, pb_ref),
        (y == 2, 0, pa_ref),
        (jnp.logical_or(y == 0, y == 3), 0, s_ref),
        (y < 2, n, pa_ref),
        (y >= 2, n, pb_ref),
    ):

        @pl.when(where)
        def _():
            out_ref[at : at + n, :] = ref[...]

    out_ref[2 * n :, :] = all_ref[n:, :]


def pick(y, s, pa, pb, rest, *after):
    n, m = s.shape
    return _call(
        _pick_kernel,
        "pick",
        moved=8 * s.size,
        in_specs=[SCALARS, FULL, FULL, FULL, FULL] + _any(len(after)),
        out_specs=FULL,
        out_shape=jax.ShapeDtypeStruct((n + rest.shape[0], m), s.dtype),
    )(y, s, pa, pb, rest, *after)


def rows_of(refs, lo, hi):
    if len(refs) == 1:
        return refs[0][lo:hi, :]
    n = refs[0].shape[0]
    parts = []
    if lo < n:
        parts.append(refs[0][lo : min(hi, n), :])
    if hi > n:
        parts.append(refs[1][max(lo, n) - n : hi - n, :])
    return parts[0] if len(parts) == 1 else jnp.concatenate(parts, axis=0)


def blocks_of(refs):
    own, one, two_lo, two_hi, three = refs
    return [own], [one], [two_lo, two_hi], [three]


PIECES = 5


ORDER = (2, 1, 3, 0)


def _update_kernel(coeff, slabs, d, rest, nb, nafter, block_ref, *refs):
    blocks = blocks_of(refs[:PIECES])
    b_refs = refs[PIECES : PIECES + nb]
    pp_ref, pm_ref, rp_ref, rm_ref, own_ref, lhs_ref = refs[PIECES + nb + nafter :]
    m = b_refs[0].shape[2]
    n = d // 2
    i = pl.program_id(0)

    @pl.when(i == 0)
    def _():
        for step in range(RING):
            for j, block in enumerate(blocks):

                @pl.when(block_ref[step] == j)
                def _():
                    for k in range(slabs):
                        lhs_ref[step * d : (step + 1) * d, k * m : (k + 1) * m] = rows_of(block, k * d, (k + 1) * d)

    def product(sides, rows):
        rhs = []
        for first in range(0, nb, 2):
            for r in range(b_refs[first].shape[0]):
                parts = [b_refs[first + side][r, :rows, :] for side in sides]
                rhs.append(parts[0] if len(parts) == 1 else jnp.concatenate(parts, axis=0))
        acc = lax.dot_general(lhs_ref[...], jnp.concatenate(rhs, axis=1), NT, preferred_element_type=f32)
        acc = (acc * coeff).astype(bf16)
        two, one, back, own = (acc[k * d : (k + 1) * d] for k in range(RING))
        w = acc.shape[1]
        pp_ref[:n, :w] = two[:n]
        pm_ref[:n, :w] = two[n:]
        pp_ref[n:, :w] = one[n:]
        rp_ref[:, :w] = one[:n]
        pm_ref[n:, :w] = back[:n]
        rm_ref[:, :w] = back[n:]
        own_ref[:, :w] = own

    size = b_refs[0].shape[1]

    @pl.when(i < 3)
    def _():
        product((0,), size)

    @pl.when(jnp.logical_and(i >= 3, i < 6))
    def _():
        product((1,), size)

    @pl.when(i == 6)
    def _():
        product((0, 1), rest)


CUT = 384


def update(coeff, block, rows, factors, seconds, *after):
    _, q, m = seconds[0].shape
    slabs = sum(b.shape[0] for b in seconds[::2])
    d = rows
    wide = 2 * q

    def once(shape):
        return pl.BlockSpec(shape, lambda i, w: (0,) * len(shape), pipeline_mode=pl.Buffered(1))

    def cut(n):
        return pl.BlockSpec((n, CUT), lambda i, w: (0, i))

    def near(b):
        return pl.BlockSpec((b.shape[0], CUT, m), lambda i, w: (0, jnp.minimum(i, 3), 0))

    def far(b):
        return pl.BlockSpec((b.shape[0], CUT, m), lambda i, w: (0, jnp.maximum(i - 3, 0), 0))

    sizes = (d, d, d // 2, d // 2, d)
    return _call(
        functools.partial(_update_kernel, coeff, slabs, d, q - 3 * CUT, len(seconds), len(after)),
        "update",
        flops=2 * RING * d * slabs * m * wide,
        moved=2 * (RING * slabs * d * m + slabs * m * wide + RING * d * wide),
        grid_spec=pltpu.PrefetchScalarGridSpec(
            num_scalar_prefetch=1,
            grid=(7,),
            in_specs=[once(f.shape) for f in factors] + [(near, far)[i % 2](b) for i, b in enumerate(seconds)] + _any(len(after)),
            out_specs=[cut(n) for n in sizes],
            scratch_shapes=[pltpu.VMEM((RING * d, slabs * m), bf16)],
        ),
        out_shape=[jax.ShapeDtypeStruct((n, wide), bf16) for n in sizes],
    )(block, *factors, *seconds, *after)


def _at(shape, row=0):
    return pl.BlockSpec(shape, lambda i: (row, 0))


def _relay_kernel(gp_ref, gm_ref, rp_ref, rm_ref, *refs):
    ap_ref, am_ref = refs[-2:]
    ap_ref[...] = (rp_ref[...].astype(f32) + gp_ref[...].astype(f32)).astype(bf16)
    am_ref[...] = (rm_ref[...].astype(f32) + gm_ref[...].astype(f32)).astype(bf16)


def relay(gp, gm, rp, rm, *after):
    spec = _at(rp.shape)
    return _call(
        _relay_kernel,
        "relay",
        grid=(1,),
        moved=12 * rp.size,
        in_specs=[spec] * 4 + _any(len(after)),
        out_specs=[spec] * 2,
        out_shape=[jax.ShapeDtypeStruct(rp.shape, bf16)] * 2,
    )(gp, gm, rp, rm, *after)


def _halves_kernel(one_ref, three_ref, *refs):
    lo_ref, hi_ref = refs[-2:]
    lo_ref[...] = one_ref[...]
    hi_ref[...] = three_ref[...]


def halves(one, three, *after):
    n, m = one.shape[0] // 2, one.shape[1]
    return _call(
        _halves_kernel,
        "halves",
        grid=(1,),
        moved=8 * n * m,
        in_specs=[_at((n, m)), _at((n, m), 1)] + _any(len(after)),
        out_specs=[_at((n, m))] * 2,
        out_shape=[jax.ShapeDtypeStruct((n, m), bf16)] * 2,
    )(one, three, *after)


def _total(own_ref, gp_ref, gm_ref, fp_ref, fm_ref):
    n = fp_ref.shape[0]
    first = own_ref[:n, :].astype(f32) + gm_ref[n:, :].astype(f32) + fp_ref[...].astype(f32)
    second = own_ref[n:, :].astype(f32) + gp_ref[n:, :].astype(f32) + fm_ref[...].astype(f32)
    return jnp.concatenate([first, second], axis=0)


def _split(total, near_ref, far_ref):
    q, k = near_ref.shape[1], 3 * CUT
    near_ref[:, :k] = total[:, :k]
    near_ref[:, k:] = total[:, 2 * k : k + q]
    far_ref[:, :k] = total[:, k : 2 * k].astype(bf16)
    far_ref[:, k:] = total[:, k + q :].astype(bf16)


def _ends(shape):
    d, q = shape[0], shape[1] // 2
    return [jax.ShapeDtypeStruct((d, q), f32), jax.ShapeDtypeStruct((d, q), bf16)]


def gate_sum(*parts):
    def kernel(*refs):
        _split(_total(*refs[:5]), *refs[5:])

    return _call(
        kernel,
        "gate_sum",
        moved=14 * parts[0].size,
        in_specs=[FULL] * 5,
        out_specs=[FULL] * 2,
        out_shape=_ends(parts[0].shape),
    )(*parts)


def _up_sums_kernel(mine_ref, *refs):
    keep_ref, send_ref = refs[10:]
    a, b = _total(*refs[:5]), _total(*refs[5:10])
    mine = mine_ref[0] == 1
    keep_ref[...] = jnp.where(mine, a, b)
    send_ref[...] = jnp.where(mine, b, a).astype(bf16)


def up_sums(mine, parts_a, parts_b, *after):
    shape = parts_a[0].shape

    def kernel(mine_ref, *refs):
        _up_sums_kernel(mine_ref, *refs[:10], *refs[-2:])

    return _call(
        kernel,
        "up_sums",
        moved=28 * parts_a[0].size,
        in_specs=[SCALARS] + [FULL] * 10 + _any(len(after)),
        out_specs=[FULL] * 2,
        out_shape=[jax.ShapeDtypeStruct(shape, f32), jax.ShapeDtypeStruct(shape, bf16)],
    )(mine, *parts_a, *parts_b, *after)


def up_sum(keep, sent):
    def kernel(keep_ref, sent_ref, near_ref, far_ref):
        _split(keep_ref[...] + sent_ref[...].astype(f32), near_ref, far_ref)

    return _call(
        kernel,
        "up_sum",
        moved=12 * keep.size,
        in_specs=[FULL] * 2,
        out_specs=[FULL] * 2,
        out_shape=_ends(keep.shape),
    )(keep, sent)


def _renew_kernel(c_ref, held_ref, near_ref, far_ref, out_ref):
    d = near_ref.shape[0]
    near, far = near_ref[...], far_ref[...].astype(f32)

    def put(first, second):
        out_ref[:d, :] = (held_ref[:d, :].astype(f32) + first).astype(bf16)
        out_ref[d:, :] = (held_ref[d:, :].astype(f32) + second).astype(bf16)

    @pl.when(c_ref[0] == 0)
    def _():
        put(near, far)

    @pl.when(c_ref[0] == 1)
    def _():
        put(far, near)


def renew(c, held, near, far):
    return _call(
        _renew_kernel,
        "renew",
        moved=6 * held.size,
        in_specs=[SCALARS] + [FULL] * 3,
        out_specs=FULL,
        out_shape=jax.ShapeDtypeStruct(held.shape, bf16),
    )(c, held, near, far)


def _tokens_kernel(n, at_ref, *refs):
    tok_ref = refs[-1]
    t, m = tok_ref.shape[1], refs[0].shape[1]
    d = (tok_ref.shape[0] - 2 * n) // (2 * RING)
    x, h = at_ref[0], at_ref[1]
    wide = t // m
    total = None
    for s in range(2):
        gather = refs[s * PIECES : (s + 1) * PIECES]
        start = gather[0].shape[0] - wide * (d + 2 * n)
        for j, block in enumerate(blocks_of(gather)):
            rows = [rows_of(block, start + i * d, start + (i + 1) * d) for i in range(wide)]
            to = 2 * lax.rem(x + RING - j, RING) + (h if s == 0 else 1 - h)
            tok_ref[pl.ds(pl.multiple_of(to * d, d), d), :] = jnp.concatenate(rows, axis=1)
            at = start + wide * d
            terms = [rows_of(block, at + i * 2 * n, at + (i + 1) * 2 * n).astype(f32) for i in range(wide)]
            both = jnp.concatenate(terms, axis=1)
            value = both[:n] + both[n:]
            total = value if total is None else total + value
    high = total.astype(bf16)
    low = (total - high.astype(f32)).astype(bf16)
    tok_ref[2 * RING * d :, :] = jnp.concatenate([high, low], axis=0)


def tokens_of(at, own, other, d, t, probes, *after):
    return _call(
        functools.partial(_tokens_kernel, probes),
        "tokens",
        moved=8 * RING * 2 * d * t,
        in_specs=[SCALARS] + [FULL] * (2 * PIECES) + _any(len(after)),
        out_specs=FULL,
        out_shape=jax.ShapeDtypeStruct((2 * RING * d + 2 * probes, t), bf16),
    )(at, *own, *other, *after)


def _hidden_kernel(c_ref, mine_ref, other_ref, wg_ref, wu_ref, bg_ref, bu_ref, *refs):
    out_ref, tok_ref, p_ref = refs[-3:]
    rank, _, m = bg_ref.shape
    t = mine_ref.shape[1]
    n = 2 * rank
    d = (mine_ref.shape[0] - 2 * n) // (2 * RING)

    @pl.when(pl.program_id(0) == 0)
    def _():
        c = c_ref[0]
        for ref, core in ((mine_ref, c), (other_ref, 1 - c)):
            for i in range(2 * RING):
                tok_ref[pl.ds(pl.multiple_of((2 * i + core) * d, d), d), :] = ref[i * d : (i + 1) * d, :]
        mask = _own_mask(m, t)
        terms = mine_ref[2 * RING * d :, :].astype(f32) + other_ref[2 * RING * d :, :].astype(f32)
        probe = (terms[:n] + terms[n:]).astype(bf16).astype(f32) * noise_scale
        for i in range(2 * rank):
            row = jnp.broadcast_to(probe[i : i + 1, :], (m, t))
            p_ref[i * m : (i + 1) * m, :] = jnp.where(mask, row, 0.0).astype(bf16)

    pre = []
    for k, (w_ref, b_ref) in enumerate(((wg_ref, bg_ref), (wu_ref, bu_ref))):
        b = jnp.concatenate([b_ref[r] for r in range(rank)], axis=1)
        acc = jnp.dot(w_ref[...], tok_ref[...], preferred_element_type=f32)
        acc += jnp.dot(b, p_ref[k * rank * m : (k + 1) * rank * m, :], preferred_element_type=f32)
        pre.append(acc)
    g, u = pre
    out_ref[...] = (g / (1.0 + jnp.exp(-g)) * u).astype(out_ref.dtype)


def hidden_of(c, mine, other, wg, wu, bg, bu, *after):
    t = mine.shape[1]
    q, d = wg.shape
    rank, _, m = bg.shape
    block = 304
    w_spec = pl.BlockSpec((block, d), lambda i: (i, 0))
    b_spec = pl.BlockSpec((rank, block, m), lambda i: (0, i, 0))
    t_spec = pl.BlockSpec(mine.shape, lambda i: (0, 0), pipeline_mode=pl.Buffered(1))
    return _call(
        _hidden_kernel,
        "hidden",
        flops=4 * q * t * (d + rank * m),
        moved=2 * (2 * q * d + d * t + 2 * rank * q * m + q * t),
        grid=(pl.cdiv(q, block),),
        in_specs=[SCALARS, t_spec, t_spec, w_spec, w_spec, b_spec, b_spec] + _any(len(after)),
        out_specs=pl.BlockSpec((block, t), lambda i: (i, 0)),
        out_shape=jax.ShapeDtypeStruct((q, t), bf16),
        scratch_shapes=[pltpu.VMEM((d, t), bf16), pltpu.VMEM((2 * rank * m, t), bf16)],
    )(c, mine, other, wg, wu, bg, bu, *after)


def local(tokens, w_gate, w_up, a_gate, a_up, b_gate, b_up, fitness):
    members, rank, d = a_gate.shape
    q = w_gate.shape[1]
    coeff = 1.0 / (members * lax.axis_size("z") * lax.axis_size("l") * rank) ** 0.5
    z, l, x, h, c = (lax.axis_index(a) for a in AXES)
    tok_t = tokens.T
    ag_t, au_t = (a.transpose(1, 2, 0) for a in (a_gate, a_up))
    bg, bu = (b.transpose(1, 2, 0) for b in (b_gate, b_up))
    block = (x - z - jnp.array(ORDER, jnp.int32)) % RING

    sg, su, rest = pack(tok_t, ag_t, au_t, fitness[None, :])
    bu_c = swap(bu, "c")

    def hop(axis, first, second):
        return swap(first, axis, 1), swap(second, axis, -1)

    one, three = hop("x", su, su)
    so = swap(rest, "h")
    first = (2 * z + l) * 2 * d
    held = [lax.dynamic_slice_in_dim(w, first, 2 * d, 0) for w in (w_gate, w_up)]
    one, three, bu_c, *held = join([one, three, bu_c, *held])
    at_y = (0, 2, 1, 3)
    sg_y = tie(sg, so)
    pa, pb = (
        lax.ppermute(sg_y, ("l", "h"), [(at_y[i], at_y[j]) for i, j in pairs])
        for pairs in (((1, 0), (2, 1), (0, 2)), ((3, 1), (1, 2), (2, 3)))
    )
    lo, hi, so = join([*hop("x", *halves(one, three)), so])
    su_x = (su, one, lo, hi, three)
    so = tie(so, lo)
    one, three = hop("x", so, so)
    ua = update(coeff, block, d, su_x, [bu, bu_c], so)
    gp_a, gm_a = hop("z", *ua[:2])
    one, three = join([one, three], ua[-1])
    lo, hi = hop("x", *halves(one, three))
    both = pick((2 * h + l).reshape(1), sg_y, pa, pb, rest, one)
    far_0 = swap(tie(bg, both), "l")
    lo, hi = join([lo, hi], both)
    so_x = (so, one, lo, hi, three)
    both = tie(both, lo)
    one, three = hop("x", both, both)
    ub = update(coeff, block, d, so_x, [bu, bu_c], both)
    gp_a, gm_a = join([gp_a, gm_a], ub[-1])
    ap, am = relay(gp_a, gm_a, *ua[2:4])
    fp_a, fm_a = hop("z", ap, am)
    one, three = join([one, three], ap, ub[-1])
    lo, hi = hop("x", *halves(one, three))
    fp_a, fm_a = join([fp_a, fm_a], one)
    gp_b, gm_b = hop("z", *join(ub[:2], fp_a))
    lo, hi = join([lo, hi], fp_a)
    sg_x = (both, one, lo, hi, three)
    bg_c = swap(tie(bg, lo), "c")
    tok = tokens_of(jnp.stack([x, h]), sg_x, so_x, d, tok_t.shape[1], 2 * rank)
    tok_c = swap(tok, "c")
    gp_b, gm_b, far_0 = join([gp_b, gm_b, far_0], tok)
    ap, am = relay(gp_b, gm_b, *ub[2:4])
    fp_b, fm_b = hop("z", ap, am)
    fars = [v for far in (far_0,) for v in (far, swap(far, "c"))]
    gg = update(coeff, block, d, sg_x, [bg, bg_c, *fars], ap)
    fp_b, fm_b = join([fp_b, fm_b], gg[-1])
    gp_g, gm_g = hop("z", *gg[:2])
    keep, send = up_sums(
        (l == h).astype(jnp.int32).reshape(1), (ua[4], gp_a, gm_a, fp_a, fm_a), (ub[4], gp_b, gm_b, fp_b, fm_b)
    )
    sent = swap(send, "l")
    hidden = hidden_of(c.reshape(1), tok, tok_c, w_gate.T, w_up.T, bg, bu, gg[-1])
    gp_g, gm_g = join([gp_g, gm_g], hidden)
    fp_g, fm_g = hop("z", *relay(gp_g, gm_g, *gg[2:4]))
    up_near, up_far = up_sum(keep, tie(sent, gp_g))
    fp_g, fm_g = join([fp_g, fm_g], up_near)
    gate_near, gate_far = gate_sum(gg[4], gp_g, gm_g, fp_g, fm_g)

    news = [
        renew(c.reshape(1), w, near, swap(far, "c"))
        for w, near, far in ((held[0], gate_near, gate_far), (held[1], up_near, up_far))
    ]
    return hidden.T, news[0], news[1]


def solution(mesh):
    fine = Mesh(mesh.devices.reshape(4, 2, 4, 2, 2), AXES)
    pop, mp = ("z", "l"), ("x", "h", "c")
    return jax.shard_map(
        local,
        mesh=fine,
        in_specs=(
            P(pop, mp),
            P(None, mp),
            P(None, mp),
            P(pop, None, mp),
            P(pop, None, mp),
            P(pop, None, mp),
            P(pop, None, mp),
            P(pop),
        ),
        out_specs=(P(pop, mp), P(pop, mp), P(pop, mp)),
        check_vma=False,
    )
```

time: 290 us -> 221 us (0.76)
  waiting for transfers between devices: 105 us -> 24.9 us
  Pallas kernels: 77.3 us -> 106 us
  starting transfers between devices: 73.2 us -> 55.3 us
  local copies, waits for them, and re-layouts: 18.8 us -> 32.6 us
  other arithmetic: 14.5 us -> 1.18 us
    ppermute x35 -> x33, waiting for transfers between devices: 105 us -> 24.9 us  [swap(): return lax.ppermute(v, axis, [(i, (i + shift) % n) for i in range(n)])]
    pallas_call x8 -> x34, Pallas kernels: 54.3 us -> 82.2 us  [the longest x3 44.2 us: update(): _call(functools.partial(_update_kernel, coeff, slabs, d, q - 3 * CUT, len...]
    unnamed x67 -> x66, local copies, waits for them, and re-layouts: 13.6 us -> 29.5 us
    ppermute x35 -> x33, starting transfers between devices: 66.9 us -> 52 us  [swap(): return lax.ppermute(v, axis, [(i, (i + shift) % n) for i in range(n)])]
    convert_element_type x8 -> x0, other arithmetic: 6 us -> none  [the longest x2 2.71 us: local(): news.append((held + both_rows).astype(bf16))]
    add x10 -> x0, other arithmetic: 5.23 us -> none  [the longest x3 2.15 us: over_z(): first = own[:n] + gm[n:].astype(f32) + fp.astype(f32)]
    ppermute x2, starting transfers between devices: 6.31 us -> 3.34 us  [local(): lax.ppermute(sg_y, ('l', 'h'), [(at_y[i], at_y[j]) for i, j in pairs])]
  transfers between devices with their start and end apart: 37 -> 35, of which waited for: 10 -> 6; matrix products, arithmetic and copies ran while one was open for 8% -> 6% of each run, Pallas kernels for 27% -> 46%
where the time goes in v3:
time: 221 us; the launch traced here: 220 us
  Pallas kernels  106 us (48%)
  starting transfers between devices  55.3 us (25%)
  local copies, waits for them, and re-layouts  32.6 us (15%)
  waiting for transfers between devices  24.9 us (11%)
    ppermute x33, starting transfers between devices, swap(): return lax.ppermute(v, axis, [(i, (i + shift) % n) for i in range(n)])  52 us
    pallas_call x3, Pallas kernels, update(): _call(functools.partial(_update_kernel, coeff, slabs, d, q - 3 * CUT, len...  44.2 us
    unnamed x66, local copies, waits for them, and re-layouts  29.5 us
    ppermute x33, waiting for transfers between devices, swap(): return lax.ppermute(v, axis, [(i, (i + shift) % n) for i in range(n)])  24.9 us
    pallas_call x1, Pallas kernels, hidden_of(): _call(_hidden_kernel, 'hidden', flops=4 * q * t * (d + rank * m), moved=2...  17.6 us
    pallas_call x3, Pallas kernels, relay(): _call(_relay_kernel, 'relay', grid=(1,), moved=12 * rp.size, in_specs=[sp...  8 us
    pallas_call x2, Pallas kernels, renew(): _call(_renew_kernel, 'renew', moved=6 * held.size, in_specs=[SCALARS] + [...  6.16 us
    pallas_call x3, Pallas kernels, halves(): _call(_halves_kernel, 'halves', grid=(1,), moved=8 * n * m, in_specs=[_at...  6.11 us
  transfers between devices with their start and end apart: 35, of which 6 were waited for; matrix products, arithmetic and copies ran while one was open for 6% of the time, Pallas kernels for 46%

profile of v3, /device:TPU:1, one launch (start us, length us, event | category | flops | bytes accessed | tf_op | source)
XLA Modules:
  0.0 220.4 jit_solution(11994187341119751417)
XLA Ops:
  0.6 1.5 collective-permute-start.5
  2.1 3.1 %pack.1 = (bf16[896,256]{1,0:T(8,128)(2,1)}, bf16[896,256]{1,0:T(8,128)(2,1)}, bf16[1376,256]{1,0:T(8,128)(2,1)}) custom-call(bf16[224,512]{1,0:T(8,128)(2,1)} %bitcast.27, bf16[4,224,256]{2,1,0:T(8,128)(2,1)} %bitcast.25, bf16[4,224,256]{2,1,0:T(8,128)(2,1)} %bitcast.26, f32[1,256]{1,0:T(1,128)} %bitcast.28), custom_call_target="tpu_custom_call" | custom-call | flops 469762048 | bytes 1835008 | tf_op jit(solution)/shard_map/pack/pallas_call | solution.py:95
  5.2 3.0 %collective-permute-start = (bf16[1376,256]{1,0:T(8,128)(2,1)}, bf16[1376,256]{1,0:T(8,128)(2,1)S(1)}, u32[]{:S(2)}, u32[]{:S(2)}) collective-permute-start(bf16[1376,256]{1,0:T(8,128)(2,1)} %get-tuple-element.71.all_ref), channel_id=1, source_target_pairs={{0,2},{2,0},{1,3},{3,1},{4,6},{6,4},{5,7},{7,5},{8,10},{10,8},{9,1... | collective-permute-start | bytes 2113544 | tf_op jit(solution)/shard_map/ppermute | solution.py:42
  8.2 1.2 collective-permute-start.3
  9.5 1.5 collective-permute-start.4
  10.9 3.2 %constant_dynamic-slice_fusion = (bf16[448,1184]{0,1:T(8,128)(2,1)S(1)}, bf16[448,1184]{0,1:T(8,128)(2,1)S(1)}) fusion(bf16[3584,1184]{0,1:T(8,128)(2,1)} %param.11, s32[]{:T(128)S(6)} %select_n.11, bf16[3584,1184]{0,1:T(8,128)(2,1)} %param.10), kind=kLoop, calls=%fused_computation.5 | loop fusion | bytes 4243460 | tf_op jit(solution)/shard_map/dynamic_slice | solution.py:496
  14.1 1.6 copy.51.refs_3_
  15.7 1.5 copy.52.refs_4_
  17.2 4.4 %collective-permute-done.3.refs_0_ = bf16[896,256]{1,0:T(8,128)(2,1)} collective-permute-done((bf16[896,256]{1,0:T(8,128)(2,1)}, bf16[896,256]{1,0:T(8,128)(2,1)}, u32[]{:S(2)}, u32[]{:S(2)}) %collective-permute-start.3) | collective-permute-done | bytes 458784 | tf_op jit(solution)/shard_map/ppermute | solution.py:42
  21.6 1.8 halves.3
  23.4 0.9 collective-permute-start.6
  24.3 1.8 collective-permute-start.7
  26.1 0.9 copy-done.2
  27.0 3.8 %collective-permute-done.6.refs_0_ = bf16[448,256]{1,0:T(8,128)(2,1)S(1)} collective-permute-done((bf16[448,256]{1,0:T(8,128)(2,1)}, bf16[448,256]{1,0:T(8,128)(2,1)S(1)}, u32[]{:S(2)}, u32[]{:S(2)}) %collective-permute-start.6) | collective-permute-done | bytes 229408 | tf_op jit(solution)/shard_map/ppermute | solution.py:42
  32.2 2.7 %collective-permute-start.9 = (bf16[1376,256]{1,0:T(8,128)(2,1)}, bf16[1376,256]{1,0:T(8,128)(2,1)S(1)}, u32[]{:S(2)}, u32[]{:S(2)}) collective-permute-start(bf16[1376,256]{1,0:T(8,128)(2,1)} %join.22.refs_7_.refs_0_.refs_5_), channel_id=1, source_target_pairs={{0,12},{4,0},{8,4},{12,8},{1,13},{5,1},{9,5},{13,9},{2,14},{6,2},{... | collective-permute-start | bytes 2113544 | tf_op jit(solution)/shard_map/ppermute | solution.py:42
  35.4 1.9 collective-permute-start.1
  37.4 1.4 collective-permute-start.2
  38.8 12.0 %update.3 = (bf16[224,2368]{1,0:T(8,128)(2,1)}, bf16[224,2368]{1,0:T(8,128)(2,1)}, bf16[112,2368]{1,0:T(8,128)(2,1)}, bf16[112,2368]{1,0:T(8,128)(2,1)}, bf16[224,2368]{1,0:T(8,128)(2,1)}) custom-call(s32[4]{0:T(128)} %and_select_fusion.block_ref, bf16[896,256]{1,0:T(8,128)(2,1)} %get-tuple-element.72.refs_0_, ...), custom_call_target="tpu_custom_call" | custom-call | flops 4345298944 | bytes 10928128 | tf_op jit(solution)/shard_map/update/pallas_call | solution.py:233
  50.8 1.8 collective-permute-start.14
  52.6 2.2 collective-permute-start.15
  54.8 0.9 copy-done.12
  55.7 2.0 halves.4
  58.4 2.7 %collective-permute-start.11 = (bf16[688,256]{1,0:T(8,128)(2,1)}, bf16[688,256]{1,0:T(8,128)(2,1)S(1)}, u32[]{:S(2)}, u32[]{:S(2)}) collective-permute-start(bf16[688,256]{1,0:T(8,128)(2,1)} %get-tuple-element.85), channel_id=1, source_target_pairs={{0,12},{4,0},{8,4},{12,8},{1,13},{5,1},{9,5},{13,9},{2,14},{6,2},{... | collective-permute-start | bytes 1056776 | tf_op jit(solution)/shard_map/ppermute | solution.py:42
  61.1 3.3 %copy.79.refs_0_ = bf16[4,1184,256]{2,1,0:T(8,128)(2,1)} copy(bf16[4,1184,256]{2,1,0:T(8,128)(2,1)} %bitcast.14) | data formatting | bytes 4849664
  64.5 2.6 %pick.1.refs_2_.refs_0_.refs_1_ = bf16[2272,256]{1,0:T(8,128)(2,1)} custom-call(s32[1]{0:T(128)} %bitcast.3.y_ref, bf16[896,256]{1,0:T(8,128)(2,1)} %join.19.s_ref, bf16[896,256]{1,0:T(8,128)(2,1)} %copy-done.27, bf16[896,256]{1,0:T(8,128)(2,1)} %collective-permute-done.2.pb_ref, bf16[1376,256]{1,0:T(8,128)(2,1)} %get-tuple-element.71.all_ref, ...), custom_call_target="tpu_custom_call" | custom-call | bytes 1835008 | tf_op jit(solution)/shard_map/pick/pallas_call | solution.py:127
  67.1 2.3 %collective-permute-start.24 = (bf16[4,1184,256]{2,1,0:T(8,128)(2,1)}, bf16[4,1184,256]{2,1,0:T(8,128)(2,1)}, u32[]{:S(2)}, u32[]{:S(2)}) collective-permute-start(bf16[4,1184,256]{2,1,0:T(8,128)(2,1)} %join.32), channel_id=1, source_target_pairs={{0,16},{16,0},{1,17},{17,1},{2,18},{18,2},{3,19},{19,3},{4,20},{20... | collective-permute-start | bytes 7274504 | tf_op jit(solution)/shard_map/ppermute | solution.py:42
  70.9 2.7 %collective-permute-start.13 = (bf16[2272,256]{1,0:T(8,128)(2,1)}, bf16[2272,256]{1,0:T(8,128)(2,1)S(1)}, u32[]{:S(2)}, u32[]{:S(2)}) collective-permute-start(bf16[2272,256]{1,0:T(8,128)(2,1)} %join.25.refs_7_.refs_0_), channel_id=1, source_target_pairs={{0,12},{4,0},{8,4},{12,8},{1,13},{5,1},{9,5},{13,9},{2,14},{6,2},{... | collective-permute-start | bytes 3489800 | tf_op jit(solution)/shard_map/ppermute | solution.py:42
  73.5 12.3 %update.4 = (bf16[224,2368]{1,0:T(8,128)(2,1)}, bf16[224,2368]{1,0:T(8,128)(2,1)}, bf16[112,2368]{1,0:T(8,128)(2,1)}, bf16[112,2368]{1,0:T(8,128)(2,1)}, bf16[224,2368]{1,0:T(8,128)(2,1)}) custom-call(s32[4]{0:T(128)} %and_select_fusion.block_ref, bf16[1376,256]{1,0:T(8,128)(2,1)} %join.22.refs_7_.refs_0_.refs_5_, ...), custom_call_target="tpu_custom_call" | custom-call | flops 4345298944 | bytes 10928128 | tf_op jit(solution)/shard_map/update/pallas_call | solution.py:233
  85.9 1.0 copy-done.8
  87.3 2.7 %relay.3 = (bf16[112,2368]{1,0:T(8,128)(2,1)}, bf16[112,2368]{1,0:T(8,128)(2,1)}) custom-call(bf16[224,2368]{1,0:T(8,128)(2,1)} %get-tuple-element.91.gp_ref.refs_1_, bf16[224,2368]{1,0:T(8,128)(2,1)} %get-tuple-element.92.gm_ref.refs_2_, bf16[112,2368]{1,0:T(8,128)(2,1)} %get-tuple-element.93.rp_ref, bf16[112,2368]{1,0:T(8,128)(2,1)} %get-tuple-element.94.rm_ref), custom_call_target="tpu_custom_call" | custom-call | bytes 3182592 | tf_op jit(solution)/shard_map/relay/pallas_call | solution.py:261
  89.9 2.7 %collective-permute-start.19 = (bf16[112,2368]{1,0:T(8,128)(2,1)}, bf16[112,2368]{1,0:T(8,128)(2,1)S(1)}, u32[]{:S(2)}, u32[]{:S(2)}) collective-permute-start(bf16[112,2368]{1,0:T(8,128)(2,1)} %get-tuple-element.100), channel_id=1, source_target_pairs={{0,96},{32,0},{64,32},{96,64},{1,97},{33,1},{65,33},{97,65},{2,98}... | collective-permute-start | bytes 1591304 | tf_op jit(solution)/shard_map/ppermute | solution.py:42
  92.6 2.5 %collective-permute-done.12.refs_0_ = bf16[2272,256]{1,0:T(8,128)(2,1)S(1)} collective-permute-done((bf16[2272,256]{1,0:T(8,128)(2,1)}, bf16[2272,256]{1,0:T(8,128)(2,1)S(1)}, u32[]{:S(2)}, u32[]{:S(2)}) %collective-permute-start.12) | collective-permute-done | bytes 1163296 | tf_op jit(solution)/shard_map/ppermute | solution.py:42
  95.1 1.0 copy-done
  96.1 1.0 copy-done.4
  97.1 3.2 %collective-permute-done.18.refs_0_ = bf16[112,2368]{1,0:T(8,128)(2,1)S(1)} collective-permute-done((bf16[112,2368]{1,0:T(8,128)(2,1)}, bf16[112,2368]{1,0:T(8,128)(2,1)S(1)}, u32[]{:S(2)}, u32[]{:S(2)}) %collective-permute-start.18) | collective-permute-done | bytes 530464 | tf_op jit(solution)/shard_map/ppermute | solution.py:42
  101.3 2.7 %collective-permute-start.23 = (bf16[224,2368]{1,0:T(8,128)(2,1)}, bf16[224,2368]{1,0:T(8,128)(2,1)S(1)}, u32[]{:S(2)}, u32[]{:S(2)}) collective-permute-start(bf16[224,2368]{1,0:T(8,128)(2,1)} %get-tuple-element.107), channel_id=1, source_target_pairs={{0,96},{32,0},{64,32},{96,64},{1,97},{33,1},{65,33},{97,65},{2,98}... | collective-permute-start | bytes 3182600 | tf_op jit(solution)/shard_map/ppermute | solution.py:42
  104.0 2.3 %halves.5 = (bf16[1136,256]{1,0:T(8,128)(2,1)}, bf16[1136,256]{1,0:T(8,128)(2,1)}) custom-call(bf16[2272,256]{1,0:T(8,128)(2,1)} %get-tuple-element.96.one_ref.refs_2_.refs_1_, bf16[2272,256]{1,0:T(8,128)(2,1)} %get-tuple-element.97.three_ref.refs_4_), custom_call_target="tpu_custom_call" | custom-call | bytes 2326528 | tf_op jit(solution)/shard_map/halves/pallas_call | solution.py:280
  106.3 2.7 %collective-permute-start.17 = (bf16[1136,256]{1,0:T(8,128)(2,1)}, bf16[1136,256]{1,0:T(8,128)(2,1)S(1)}, u32[]{:S(2)}, u32[]{:S(2)}) collective-permute-start(bf16[1136,256]{1,0:T(8,128)(2,1)} %get-tuple-element.99), channel_id=1, source_target_pairs={{0,12},{4,0},{8,4},{12,8},{1,13},{5,1},{9,5},{13,9},{2,14},{6,2},{... | collective-permute-start | bytes 1744904 | tf_op jit(solution)/shard_map/ppermute | solution.py:42
  109.0 1.5 copy.76.refs_0_
  111.1 5.6 %collective-permute-done.16.refs_0_ = bf16[1136,256]{1,0:T(8,128)(2,1)S(1)} collective-permute-done((bf16[1136,256]{1,0:T(8,128)(2,1)}, bf16[1136,256]{1,0:T(8,128)(2,1)S(1)}, u32[]{:S(2)}, u32[]{:S(2)}) %collective-permute-start.16) | collective-permute-done | bytes 581664 | tf_op jit(solution)/shard_map/ppermute | solution.py:42
  116.7 0.8 copy-done.13
  118.4 7.4 %collective-permute-start.21 = (bf16[4,1184,256]{2,1,0:T(8,128)(2,1)}, bf16[4,1184,256]{2,1,0:T(8,128)(2,1)S(1)}, u32[]{:S(2)}, u32[]{:S(2)}) collective-permute-start(bf16[4,1184,256]{2,1,0:T(8,128)(2,1)} %join.30), channel_id=1, source_target_pairs={{0,1},{1,0},{2,3},{3,2},{4,5},{5,4},{6,7},{7,6},{8,9},{9,8},{10,11... | collective-permute-start | bytes 7274504 | tf_op jit(solution)/shard_map/ppermute | solution.py:42
  125.8 4.5 %tokens.1.refs_3_.mine_ref = bf16[1808,512]{1,0:T(8,128)(2,1)} custom-call(s32[2]{0:T(128)} %pad_add_fusion.at_ref, bf16[2272,256]{1,0:T(8,128)(2,1)} %join.25.refs_7_.refs_0_, bf16[2272,256]{1,0:T(8,128)(2,1)} %get-tuple-element.96.one_ref.refs_2_.refs_1_, bf16[1136,256]{1,0:T(8,128)(2,1)} %get-tuple-element.102.refs_2_.refs_1_, ...), custom_call_target="tpu_custom_call" | custom-call | bytes 7340032 | tf_op jit(solution)/shard_map/tokens/pallas_call | solution.py:416
  130.3 1.0 copy-done.6
  131.3 1.0 copy-done.7
  132.8 2.7 %relay.4 = (bf16[112,2368]{1,0:T(8,128)(2,1)}, bf16[112,2368]{1,0:T(8,128)(2,1)}) custom-call(bf16[224,2368]{1,0:T(8,128)(2,1)} %get-tuple-element.109.gp_ref.refs_6_, bf16[224,2368]{1,0:T(8,128)(2,1)} %get-tuple-element.110.gm_ref.refs_7_, bf16[112,2368]{1,0:T(8,128)(2,1)} %get-tuple-element.111.rp_ref, bf16[112,2368]{1,0:T(8,128)(2,1)} %get-tuple-element.112.rm_ref), custom_call_target="tpu_custom_call" | custom-call | bytes 3182592 | tf_op jit(solution)/shard_map/relay/pallas_call | solution.py:261
  135.5 2.7 %collective-permute-start.31 = (bf16[112,2368]{1,0:T(8,128)(2,1)}, bf16[112,2368]{1,0:T(8,128)(2,1)S(1)}, u32[]{:S(2)}, u32[]{:S(2)}) collective-permute-start(bf16[112,2368]{1,0:T(8,128)(2,1)} %get-tuple-element.125), channel_id=1, source_target_pairs={{0,96},{32,0},{64,32},{96,64},{1,97},{33,1},{65,33},{97,65},{2,98}... | collective-permute-start | bytes 1591304 | tf_op jit(solution)/shard_map/ppermute | solution.py:42
  138.2 1.5 copy-done.29
  139.7 19.8 %update.5 = (bf16[224,2368]{1,0:T(8,128)(2,1)}, bf16[224,2368]{1,0:T(8,128)(2,1)}, bf16[112,2368]{1,0:T(8,128)(2,1)}, bf16[112,2368]{1,0:T(8,128)(2,1)}, bf16[224,2368]{1,0:T(8,128)(2,1)}) custom-call(s32[4]{0:T(128)} %and_select_fusion.block_ref, bf16[2272,256]{1,0:T(8,128)(2,1)} %join.25.refs_7_.refs_0_, ...), custom_call_target="tpu_custom_call" | custom-call | flops 8690597888 | bytes 17612800 | tf_op jit(solution)/shard_map/update/pallas_call | solution.py:233
  159.6 2.7 %collective-permute-start.27 = (bf16[224,2368]{1,0:T(8,128)(2,1)}, bf16[224,2368]{1,0:T(8,128)(2,1)S(1)}, u32[]{:S(2)}, u32[]{:S(2)}) collective-permute-start(bf16[224,2368]{1,0:T(8,128)(2,1)} %get-tuple-element.117), channel_id=1, source_target_pairs={{0,96},{32,0},{64,32},{96,64},{1,97},{33,1},{65,33},{97,65},{2,98}... | collective-permute-start | bytes 3182600 | tf_op jit(solution)/shard_map/ppermute | solution.py:42
  163.3 5.9 %up_sums.1 = (f32[224,2368]{1,0:T(8,128)}, bf16[224,2368]{1,0:T(8,128)(2,1)}) custom-call(s32[1]{0:T(128)} %bitcast.13.mine_ref, bf16[224,2368]{1,0:T(8,128)(2,1)} %get-tuple-element.81.refs_2_.refs_0_, bf16[224,2368]{1,0:T(8,128)(2,1)} %get-tuple-element.91.gp_ref.refs_1_, bf16[224,2368]{1,0:T(8,128)(2,1)} %get-tuple-element.92.gm_ref.refs_2_, ...), custom_call_target="tpu_custom_call" | custom-call | bytes 14852096 | tf_op jit(solution)/shard_map/up_sums/pallas_call | solution.py:339
  169.2 17.6 %hidden.1.refs_2_ = bf16[1184,512]{1,0:T(8,128)(2,1)} custom-call(s32[1]{0:T(128)} %bitcast.c_ref, bf16[1808,512]{1,0:T(8,128)(2,1)} %tokens.1.refs_3_.mine_ref, bf16[1808,512]{1,0:T(8,128)(2,1)} %collective-permute-done.20.other_ref, bf16[1184,3584]{1,0:T(8,128)(2,1)} %bitcast.20, bf16[1184,3584]{1,0:T(8,128)(2,1)} %bitcast.19, ...), custom_call_target="tpu_custom_call" | custom-call | flops 11173625856 | bytes 26705920 | tf_op jit(solution)/shard_map/hidden/pallas_call | solution.py:464
  186.8 1.0 copy-done.1
  187.8 1.0 copy-done.5
  188.8 2.6 %relay.5 = (bf16[112,2368]{1,0:T(8,128)(2,1)}, bf16[112,2368]{1,0:T(8,128)(2,1)}) custom-call(bf16[224,2368]{1,0:T(8,128)(2,1)} %get-tuple-element.118.gp_ref.refs_1_, bf16[224,2368]{1,0:T(8,128)(2,1)} %get-tuple-element.119.gm_ref.refs_2_, bf16[112,2368]{1,0:T(8,128)(2,1)} %get-tuple-element.120.rp_ref, bf16[112,2368]{1,0:T(8,128)(2,1)} %get-tuple-element.121.rm_ref), custom_call_target="tpu_custom_call" | custom-call | bytes 3182592 | tf_op jit(solution)/shard_map/relay/pallas_call | solution.py:261
  191.4 2.7 %collective-permute-start.29 = (bf16[112,2368]{1,0:T(8,128)(2,1)}, bf16[112,2368]{1,0:T(8,128)(2,1)S(1)}, u32[]{:S(2)}, u32[]{:S(2)}) collective-permute-start(bf16[112,2368]{1,0:T(8,128)(2,1)} %get-tuple-element.123), channel_id=1, source_target_pairs={{0,96},{32,0},{64,32},{96,64},{1,97},{33,1},{65,33},{97,65},{2,98}... | collective-permute-start | bytes 1591304 | tf_op jit(solution)/shard_map/ppermute | solution.py:42
  194.1 1.0 copy-done.14
  195.1 3.3 %up_sum.1 = (f32[224,1184]{1,0:T(8,128)}, bf16[224,1184]{1,0:T(8,128)(2,1)}) custom-call(f32[224,2368]{1,0:T(8,128)} %get-tuple-element.128.keep_ref, bf16[224,2368]{1,0:T(8,128)(2,1)} %join.36.sent_ref), custom_call_target="tpu_custom_call" | custom-call | bytes 6365184 | tf_op jit(solution)/shard_map/up_sum/pallas_call | solution.py:353
  198.4 1.8 collective-permute-start.34
  200.1 5.4 %collective-permute-done.28.refs_0_ = bf16[112,2368]{1,0:T(8,128)(2,1)S(1)} collective-permute-done((bf16[112,2368]{1,0:T(8,128)(2,1)}, bf16[112,2368]{1,0:T(8,128)(2,1)S(1)}, u32[]{:S(2)}, u32[]{:S(2)}) %collective-permute-start.28) | collective-permute-done | bytes 530464 | tf_op jit(solution)/shard_map/ppermute | solution.py:42
  206.5 4.0 %gate_sum.1 = (f32[224,1184]{1,0:T(8,128)}, bf16[224,1184]{1,0:T(8,128)(2,1)}) custom-call(bf16[224,2368]{1,0:T(8,128)(2,1)} %get-tuple-element.114.refs_0_.refs_2_, bf16[224,2368]{1,0:T(8,128)(2,1)} %get-tuple-element.118.gp_ref.refs_1_, bf16[224,2368]{1,0:T(8,128)(2,1)} %get-tuple-element.119.gm_ref.refs_2_, bf16[112,2368]{1,0:T(8,128)(2,1)} %get-tuple-element.131.refs_3_, ...), custom_call_target="tpu_custom_call" | custom-call | bytes 7426048 | tf_op jit(solution)/shard_map/gate_sum/pallas_call | solution.py:315
  210.5 2.1 collective-permute-start.33
  213.4 3.1 %renew.3 = bf16[448,1184]{1,0:T(8,128)(2,1)} custom-call(s32[1]{0:T(128)} %bitcast.c_ref, bf16[448,1184]{1,0:T(8,128)(2,1)} %get-tuple-element.135.held_ref, f32[224,1184]{1,0:T(8,128)} %get-tuple-element.130.refs_2_.near_ref, bf16[224,1184]{1,0:T(8,128)(2,1)} %copy-done.25), custom_call_target="tpu_custom_call" | custom-call | bytes 3182592 | tf_op jit(solution)/shard_map/renew/pallas_call | solution.py:381
  217.3 3.1 %renew.2 = bf16[448,1184]{1,0:T(8,128)(2,1)} custom-call(s32[1]{0:T(128)} %bitcast.c_ref, bf16[448,1184]{1,0:T(8,128)(2,1)} %get-tuple-element.115.held_ref, f32[224,1184]{1,0:T(8,128)} %get-tuple-element.133.near_ref, bf16[224,1184]{1,0:T(8,128)(2,1)} %copy-done.26), custom_call_target="tpu_custom_call" | custom-call | bytes 3182592 | tf_op jit(solution)/shard_map/renew/pallas_call | solution.py:381
  (112 shorter events, 11.4 us)
Async XLA Ops:
  0.6 20.9 %collective-permute-start.5 = (bf16[4,1184,256]{2,1,0:T(8,128)(2,1)}, bf16[4,1184,256]{2,1,0:T(8,128)(2,1)}, u32[]{:S(2)}, u32[]{:S(2)}) collective-permute-start(bf16[4,1184,256]{2,1,0:T(8,128)(2,1)} %bitcast.21), channel_id=1, source_target_pairs={{0,1},{1,0},{2,3},{3,2},{4,5},{5,4},{6,7},{7,6},{8,9},{9,8},{10,11... | collective-permute-start | bytes 7274504 | tf_op jit(solution)/shard_map/ppermute | solution.py:42
  5.2 20.8 %collective-permute-start = (bf16[1376,256]{1,0:T(8,128)(2,1)}, bf16[1376,256]{1,0:T(8,128)(2,1)S(1)}, u32[]{:S(2)}, u32[]{:S(2)}) collective-permute-start(bf16[1376,256]{1,0:T(8,128)(2,1)} %get-tuple-element.71.all_ref), channel_id=1, source_target_pairs={{0,2},{2,0},{1,3},{3,1},{4,6},{6,4},{5,7},{7,5},{8,10},{10,8},{9,1... | collective-permute-start | bytes 2113544 | tf_op jit(solution)/shard_map/ppermute | solution.py:42
  8.2 13.3 %collective-permute-start.3 = (bf16[896,256]{1,0:T(8,128)(2,1)}, bf16[896,256]{1,0:T(8,128)(2,1)}, u32[]{:S(2)}, u32[]{:S(2)}) collective-permute-start(bf16[896,256]{1,0:T(8,128)(2,1)} %get-tuple-element.72.refs_0_), channel_id=1, source_target_pairs={{0,4},{4,8},{8,12},{12,0},{1,5},{5,9},{9,13},{13,1},{2,6},{6,10},{... | collective-permute-start | bytes 1376264 | tf_op jit(solution)/shard_map/ppermute | solution.py:42
  9.5 12.1 %collective-permute-start.4 = (bf16[896,256]{1,0:T(8,128)(2,1)}, bf16[896,256]{1,0:T(8,128)(2,1)}, u32[]{:S(2)}, u32[]{:S(2)}) collective-permute-start(bf16[896,256]{1,0:T(8,128)(2,1)} %get-tuple-element.72.refs_0_), channel_id=1, source_target_pairs={{0,12},{4,0},{8,4},{12,8},{1,13},{5,1},{9,5},{13,9},{2,14},{6,2},{... | collective-permute-start | bytes 1376264 | tf_op jit(solution)/shard_map/ppermute | solution.py:42
  23.4 7.4 %collective-permute-start.6 = (bf16[448,256]{1,0:T(8,128)(2,1)}, bf16[448,256]{1,0:T(8,128)(2,1)S(1)}, u32[]{:S(2)}, u32[]{:S(2)}) collective-permute-start(bf16[448,256]{1,0:T(8,128)(2,1)} %get-tuple-element.75), channel_id=1, source_target_pairs={{0,4},{4,8},{8,12},{12,0},{1,5},{5,9},{9,13},{13,1},{2,6},{6,10},{... | collective-permute-start | bytes 688136 | tf_op jit(solution)/shard_map/ppermute | solution.py:42
  24.3 6.5 %collective-permute-start.7 = (bf16[448,256]{1,0:T(8,128)(2,1)}, bf16[448,256]{1,0:T(8,128)(2,1)S(1)}, u32[]{:S(2)}, u32[]{:S(2)}) collective-permute-start(bf16[448,256]{1,0:T(8,128)(2,1)} %get-tuple-element.76), channel_id=1, source_target_pairs={{0,12},{4,0},{8,4},{12,8},{1,13},{5,1},{9,5},{13,9},{2,14},{6,2},{... | collective-permute-start | bytes 688136 | tf_op jit(solution)/shard_map/ppermute | solution.py:42
  26.1 0.9 copy-start.2
  27.0 7.9 %copy-start.30 = (s32[4]{0:T(128)S(1)}, s32[4]{0:T(128)}, u32[]{:S(2)}) copy-start(s32[4]{0:T(128)} %constant.45) | copy-start | bytes 52
  27.0 8.5 %copy-start.22 = (bf16[896,256]{1,0:T(8,128)(2,1)S(1)}, bf16[896,256]{1,0:T(8,128)(2,1)}, u32[]{:S(2)}) copy-start(bf16[896,256]{1,0:T(8,128)(2,1)} %join.19.s_ref) | copy-start | bytes 1376260
  32.2 20.4 %collective-permute-start.8 = (bf16[1376,256]{1,0:T(8,128)(2,1)}, bf16[1376,256]{1,0:T(8,128)(2,1)S(1)}, u32[]{:S(2)}, u32[]{:S(2)}) collective-permute-start(bf16[1376,256]{1,0:T(8,128)(2,1)} %join.22.refs_7_.refs_0_.refs_5_), channel_id=1, source_target_pairs={{0,4},{4,8},{8,12},{12,0},{1,5},{5,9},{9,13},{13,1},{2,6},{6,10},{... | collective-permute-start | bytes 2113544 | tf_op jit(solution)/shard_map/ppermute | solution.py:42
  32.2 22.6 %collective-permute-start.9 = (bf16[1376,256]{1,0:T(8,128)(2,1)}, bf16[1376,256]{1,0:T(8,128)(2,1)S(1)}, u32[]{:S(2)}, u32[]{:S(2)}) collective-permute-start(bf16[1376,256]{1,0:T(8,128)(2,1)} %join.22.refs_7_.refs_0_.refs_5_), channel_id=1, source_target_pairs={{0,12},{4,0},{8,4},{12,8},{1,13},{5,1},{9,5},{13,9},{2,14},{6,2},{... | collective-permute-start | bytes 2113544 | tf_op jit(solution)/shard_map/ppermute | solution.py:42
  35.4 22.2 %collective-permute-start.1 = (bf16[896,256]{1,0:T(8,128)(2,1)S(1)}, bf16[896,256]{1,0:T(8,128)(2,1)S(1)}, u32[]{:S(2)}, u32[]{:S(2)}) collective-permute-start(bf16[896,256]{1,0:T(8,128)(2,1)S(1)} %copy-done.22), channel_id=1, source_target_pairs={{16,0},{2,16},{0,2},{17,1},{3,17},{1,3},{20,4},{6,20},{4,6},{21,5}... | collective-permute-start | bytes 1376264 | tf_op jit(solution)/shard_map/ppermute | solution.py:501
  37.4 27.1 %collective-permute-start.2 = (bf16[896,256]{1,0:T(8,128)(2,1)S(1)}, bf16[896,256]{1,0:T(8,128)(2,1)}, u32[]{:S(2)}, u32[]{:S(2)}) collective-permute-start(bf16[896,256]{1,0:T(8,128)(2,1)S(1)} %copy-done.22), channel_id=1, source_target_pairs={{18,16},{16,2},{2,18},{19,17},{17,3},{3,19},{22,20},{20,6},{6,22},... | collective-permute-start | bytes 1376264 | tf_op jit(solution)/shard_map/ppermute | solution.py:501
  50.8 35.1 %collective-permute-start.14 = (bf16[224,2368]{1,0:T(8,128)(2,1)}, bf16[224,2368]{1,0:T(8,128)(2,1)S(1)}, u32[]{:S(2)}, u32[]{:S(2)}) collective-permute-start(bf16[224,2368]{1,0:T(8,128)(2,1)} %get-tuple-element.87), channel_id=1, source_target_pairs={{0,32},{32,64},{64,96},{96,0},{1,33},{33,65},{65,97},{97,1},{2,34}... | collective-permute-start | bytes 3182600 | tf_op jit(solution)/shard_map/ppermute | solution.py:42
  52.6 2.2 copy-start.3
  52.6 33.3 %collective-permute-start.15 = (bf16[224,2368]{1,0:T(8,128)(2,1)}, bf16[224,2368]{1,0:T(8,128)(2,1)S(1)}, u32[]{:S(2)}, u32[]{:S(2)}) collective-permute-start(bf16[224,2368]{1,0:T(8,128)(2,1)} %get-tuple-element.88), channel_id=1, source_target_pairs={{0,96},{32,0},{64,32},{96,64},{1,97},{33,1},{65,33},{97,65},{2,98}... | collective-permute-start | bytes 3182600 | tf_op jit(solution)/shard_map/ppermute | solution.py:42
  54.8 0.9 copy-start.12
  57.6 11.7 %collective-permute-start.10 = (bf16[688,256]{1,0:T(8,128)(2,1)}, bf16[688,256]{1,0:T(8,128)(2,1)S(1)}, u32[]{:S(2)}, u32[]{:S(2)}) collective-permute-start(bf16[688,256]{1,0:T(8,128)(2,1)} %get-tuple-element.84), channel_id=1, source_target_pairs={{0,4},{4,8},{8,12},{12,0},{1,5},{5,9},{9,13},{13,1},{2,6},{6,10},{... | collective-permute-start | bytes 1056776 | tf_op jit(solution)/shard_map/ppermute | solution.py:42
  57.7 0.8 copy-start.27
  58.4 10.9 %collective-permute-start.11 = (bf16[688,256]{1,0:T(8,128)(2,1)}, bf16[688,256]{1,0:T(8,128)(2,1)S(1)}, u32[]{:S(2)}, u32[]{:S(2)}) collective-permute-start(bf16[688,256]{1,0:T(8,128)(2,1)} %get-tuple-element.85), channel_id=1, source_target_pairs={{0,12},{4,0},{8,4},{12,8},{1,13},{5,1},{9,5},{13,9},{2,14},{6,2},{... | collective-permute-start | bytes 1056776 | tf_op jit(solution)/shard_map/ppermute | solution.py:42
  67.1 63.2 %collective-permute-start.24 = (bf16[4,1184,256]{2,1,0:T(8,128)(2,1)}, bf16[4,1184,256]{2,1,0:T(8,128)(2,1)}, u32[]{:S(2)}, u32[]{:S(2)}) collective-permute-start(bf16[4,1184,256]{2,1,0:T(8,128)(2,1)} %join.32), channel_id=1, source_target_pairs={{0,16},{16,0},{1,17},{17,1},{2,18},{18,2},{3,19},{19,3},{4,20},{20... | collective-permute-start | bytes 7274504 | tf_op jit(solution)/shard_map/ppermute | solution.py:42
  69.4 0.7 copy-start.15
  70.1 0.7 copy-start.23
  70.9 24.2 %collective-permute-start.12 = (bf16[2272,256]{1,0:T(8,128)(2,1)}, bf16[2272,256]{1,0:T(8,128)(2,1)S(1)}, u32[]{:S(2)}, u32[]{:S(2)}) collective-permute-start(bf16[2272,256]{1,0:T(8,128)(2,1)} %join.25.refs_7_.refs_0_), channel_id=1, source_target_pairs={{0,4},{4,8},{8,12},{12,0},{1,5},{5,9},{9,13},{13,1},{2,6},{6,10},{... | collective-permute-start | bytes 3489800 | tf_op jit(solution)/shard_map/ppermute | solution.py:42
  70.9 24.2 %collective-permute-start.13 = (bf16[2272,256]{1,0:T(8,128)(2,1)}, bf16[2272,256]{1,0:T(8,128)(2,1)S(1)}, u32[]{:S(2)}, u32[]{:S(2)}) collective-permute-start(bf16[2272,256]{1,0:T(8,128)(2,1)} %join.25.refs_7_.refs_0_), channel_id=1, source_target_pairs={{0,12},{4,0},{8,4},{12,8},{1,13},{5,1},{9,5},{13,9},{2,14},{6,2},{... | collective-permute-start | bytes 3489800 | tf_op jit(solution)/shard_map/ppermute | solution.py:42
  85.9 1.0 copy-start.8
  85.9 1.4 copy-start.9
  89.9 10.4 %collective-permute-start.18 = (bf16[112,2368]{1,0:T(8,128)(2,1)}, bf16[112,2368]{1,0:T(8,128)(2,1)S(1)}, u32[]{:S(2)}, u32[]{:S(2)}) collective-permute-start(bf16[112,2368]{1,0:T(8,128)(2,1)} %get-tuple-element.95.refs_2_), channel_id=1, source_target_pairs={{0,32},{32,64},{64,96},{96,0},{1,33},{33,65},{65,97},{97,1},{2,34}... | collective-permute-start | bytes 1591304 | tf_op jit(solution)/shard_map/ppermute | solution.py:42
  89.9 10.4 %collective-permute-start.19 = (bf16[112,2368]{1,0:T(8,128)(2,1)}, bf16[112,2368]{1,0:T(8,128)(2,1)S(1)}, u32[]{:S(2)}, u32[]{:S(2)}) collective-permute-start(bf16[112,2368]{1,0:T(8,128)(2,1)} %get-tuple-element.100), channel_id=1, source_target_pairs={{0,96},{32,0},{64,32},{96,64},{1,97},{33,1},{65,33},{97,65},{2,98}... | collective-permute-start | bytes 1591304 | tf_op jit(solution)/shard_map/ppermute | solution.py:42
  95.1 1.0 copy-start
  96.1 1.0 copy-start.4
  100.3 0.8 copy-start.11
  100.3 1.0 copy-start.19
  101.3 7.7 %copy-start.10 = (bf16[256,4,1184]{0,2,1:T(8,128)(2,1)S(1)}, bf16[256,4,1184]{0,2,1:T(8,128)(2,1)}, u32[]{:S(2)}) copy-start(bf16[256,4,1184]{0,2,1:T(8,128)(2,1)} %param.14) | copy-start | bytes 7274500
  101.3 29.0 %collective-permute-start.22 = (bf16[224,2368]{1,0:T(8,128)(2,1)}, bf16[224,2368]{1,0:T(8,128)(2,1)S(1)}, u32[]{:S(2)}, u32[]{:S(2)}) collective-permute-start(bf16[224,2368]{1,0:T(8,128)(2,1)} %get-tuple-element.106), channel_id=1, source_target_pairs={{0,32},{32,64},{64,96},{96,0},{1,33},{33,65},{65,97},{97,1},{2,34}... | collective-permute-start | bytes 3182600 | tf_op jit(solution)/shard_map/ppermute | solution.py:42
  101.3 29.0 %collective-permute-start.23 = (bf16[224,2368]{1,0:T(8,128)(2,1)}, bf16[224,2368]{1,0:T(8,128)(2,1)S(1)}, u32[]{:S(2)}, u32[]{:S(2)}) collective-permute-start(bf16[224,2368]{1,0:T(8,128)(2,1)} %get-tuple-element.107), channel_id=1, source_target_pairs={{0,96},{32,0},{64,32},{96,64},{1,97},{33,1},{65,33},{97,65},{2,98}... | collective-permute-start | bytes 3182600 | tf_op jit(solution)/shard_map/ppermute | solution.py:42
  106.3 10.4 %collective-permute-start.16 = (bf16[1136,256]{1,0:T(8,128)(2,1)}, bf16[1136,256]{1,0:T(8,128)(2,1)S(1)}, u32[]{:S(2)}, u32[]{:S(2)}) collective-permute-start(bf16[1136,256]{1,0:T(8,128)(2,1)} %get-tuple-element.98), channel_id=1, source_target_pairs={{0,4},{4,8},{8,12},{12,0},{1,5},{5,9},{9,13},{13,1},{2,6},{6,10},{... | collective-permute-start | bytes 1744904 | tf_op jit(solution)/shard_map/ppermute | solution.py:42
  106.3 10.4 %collective-permute-start.17 = (bf16[1136,256]{1,0:T(8,128)(2,1)}, bf16[1136,256]{1,0:T(8,128)(2,1)S(1)}, u32[]{:S(2)}, u32[]{:S(2)}) collective-permute-start(bf16[1136,256]{1,0:T(8,128)(2,1)} %get-tuple-element.99), channel_id=1, source_target_pairs={{0,12},{4,0},{8,4},{12,8},{1,13},{5,1},{9,5},{13,9},{2,14},{6,2},{... | collective-permute-start | bytes 1744904 | tf_op jit(solution)/shard_map/ppermute | solution.py:42
  116.7 0.9 copy-start.13
  117.5 0.8 copy-start.16
  118.4 19.8 %collective-permute-start.21 = (bf16[4,1184,256]{2,1,0:T(8,128)(2,1)}, bf16[4,1184,256]{2,1,0:T(8,128)(2,1)S(1)}, u32[]{:S(2)}, u32[]{:S(2)}) collective-permute-start(bf16[4,1184,256]{2,1,0:T(8,128)(2,1)} %join.30), channel_id=1, source_target_pairs={{0,1},{1,0},{2,3},{3,2},{4,5},{5,4},{6,7},{7,6},{8,9},{9,8},{10,11... | collective-permute-start | bytes 7274504 | tf_op jit(solution)/shard_map/ppermute | solution.py:42
  130.3 1.0 copy-start.6
  131.3 1.0 copy-start.7
  132.3 5.9 %collective-permute-start.25 = (bf16[4,1184,256]{2,1,0:T(8,128)(2,1)}, bf16[4,1184,256]{2,1,0:T(8,128)(2,1)}, u32[]{:S(2)}, u32[]{:S(2)}) collective-permute-start(bf16[4,1184,256]{2,1,0:T(8,128)(2,1)} %get-tuple-element.108.refs_7_), channel_id=1, source_target_pairs={{0,1},{1,0},{2,3},{3,2},{4,5},{5,4},{6,7},{7,6},{8,9},{9,8},{10,11... | collective-permute-start | bytes 7274504 | tf_op jit(solution)/shard_map/ppermute | solution.py:42
  132.3 36.9 %collective-permute-start.20 = (bf16[1808,512]{1,0:T(8,128)(2,1)}, bf16[1808,512]{1,0:T(8,128)(2,1)}, u32[]{:S(2)}, u32[]{:S(2)}) collective-permute-start(bf16[1808,512]{1,0:T(8,128)(2,1)} %tokens.1.refs_3_.mine_ref), channel_id=1, source_target_pairs={{0,1},{1,0},{2,3},{3,2},{4,5},{5,4},{6,7},{7,6},{8,9},{9,8},{10,11... | collective-permute-start | bytes 5554184 | tf_op jit(solution)/shard_map/ppermute | solution.py:42
  135.5 26.7 %collective-permute-start.30 = (bf16[112,2368]{1,0:T(8,128)(2,1)}, bf16[112,2368]{1,0:T(8,128)(2,1)S(1)}, u32[]{:S(2)}, u32[]{:S(2)}) collective-permute-start(bf16[112,2368]{1,0:T(8,128)(2,1)} %get-tuple-element.113.refs_9_), channel_id=1, source_target_pairs={{0,32},{32,64},{64,96},{96,0},{1,33},{33,65},{65,97},{97,1},{2,34}... | collective-permute-start | bytes 1591304 | tf_op jit(solution)/shard_map/ppermute | solution.py:42
  135.5 26.7 %collective-permute-start.31 = (bf16[112,2368]{1,0:T(8,128)(2,1)}, bf16[112,2368]{1,0:T(8,128)(2,1)S(1)}, u32[]{:S(2)}, u32[]{:S(2)}) collective-permute-start(bf16[112,2368]{1,0:T(8,128)(2,1)} %get-tuple-element.125), channel_id=1, source_target_pairs={{0,96},{32,0},{64,32},{96,64},{1,97},{33,1},{65,33},{97,65},{2,98}... | collective-permute-start | bytes 1591304 | tf_op jit(solution)/shard_map/ppermute | solution.py:42
  138.2 1.5 copy-start.29
  159.5 27.3 %collective-permute-start.26 = (bf16[224,2368]{1,0:T(8,128)(2,1)}, bf16[224,2368]{1,0:T(8,128)(2,1)S(1)}, u32[]{:S(2)}, u32[]{:S(2)}) collective-permute-start(bf16[224,2368]{1,0:T(8,128)(2,1)} %get-tuple-element.116), channel_id=1, source_target_pairs={{0,32},{32,64},{64,96},{96,0},{1,33},{33,65},{65,97},{97,1},{2,34}... | collective-permute-start | bytes 3182600 | tf_op jit(solution)/shard_map/ppermute | solution.py:42
  159.6 27.2 %collective-permute-start.27 = (bf16[224,2368]{1,0:T(8,128)(2,1)}, bf16[224,2368]{1,0:T(8,128)(2,1)S(1)}, u32[]{:S(2)}, u32[]{:S(2)}) collective-permute-start(bf16[224,2368]{1,0:T(8,128)(2,1)} %get-tuple-element.117), channel_id=1, source_target_pairs={{0,96},{32,0},{64,32},{96,64},{1,97},{33,1},{65,33},{97,65},{2,98}... | collective-permute-start | bytes 3182600 | tf_op jit(solution)/shard_map/ppermute | solution.py:42
  162.3 0.8 copy-start.17
  162.3 1.0 copy-start.18
  169.2 24.9 %collective-permute-start.32 = (bf16[224,2368]{1,0:T(8,128)(2,1)}, bf16[224,2368]{1,0:T(8,128)(2,1)S(1)}, u32[]{:S(2)}, u32[]{:S(2)}) collective-permute-start(bf16[224,2368]{1,0:T(8,128)(2,1)} %get-tuple-element.129), channel_id=1, source_target_pairs={{0,16},{16,0},{1,17},{17,1},{2,18},{18,2},{3,19},{19,3},{4,20},{20... | collective-permute-start | bytes 3182600 | tf_op jit(solution)/shard_map/ppermute | solution.py:42
  186.8 1.0 copy-start.1
  187.8 1.0 copy-start.5
  191.4 14.1 %collective-permute-start.28 = (bf16[112,2368]{1,0:T(8,128)(2,1)}, bf16[112,2368]{1,0:T(8,128)(2,1)S(1)}, u32[]{:S(2)}, u32[]{:S(2)}) collective-permute-start(bf16[112,2368]{1,0:T(8,128)(2,1)} %get-tuple-element.122), channel_id=1, source_target_pairs={{0,32},{32,64},{64,96},{96,0},{1,33},{33,65},{65,97},{97,1},{2,34}... | collective-permute-start | bytes 1591304 | tf_op jit(solution)/shard_map/ppermute | solution.py:42
  191.4 14.1 %collective-permute-start.29 = (bf16[112,2368]{1,0:T(8,128)(2,1)}, bf16[112,2368]{1,0:T(8,128)(2,1)S(1)}, u32[]{:S(2)}, u32[]{:S(2)}) collective-permute-start(bf16[112,2368]{1,0:T(8,128)(2,1)} %get-tuple-element.123), channel_id=1, source_target_pairs={{0,96},{32,0},{64,32},{96,64},{1,97},{33,1},{65,33},{97,65},{2,98}... | collective-permute-start | bytes 1591304 | tf_op jit(solution)/shard_map/ppermute | solution.py:42
  194.1 1.0 copy-start.14
  198.4 14.2 %collective-permute-start.34 = (bf16[224,1184]{1,0:T(8,128)(2,1)}, bf16[224,1184]{1,0:T(8,128)(2,1)S(1)}, u32[]{:S(2)}, u32[]{:S(2)}) collective-permute-start(bf16[224,1184]{1,0:T(8,128)(2,1)} %get-tuple-element.136), channel_id=1, source_target_pairs={{0,1},{1,0},{2,3},{3,2},{4,5},{5,4},{6,7},{7,6},{8,9},{9,8},{10,11... | collective-permute-start | bytes 1591304 | tf_op jit(solution)/shard_map/ppermute | solution.py:42
  205.5 0.8 copy-start.20
  205.5 1.0 copy-start.21
  210.5 6.0 %collective-permute-start.33 = (bf16[224,1184]{1,0:T(8,128)(2,1)}, bf16[224,1184]{1,0:T(8,128)(2,1)S(1)}, u32[]{:S(2)}, u32[]{:S(2)}) collective-permute-start(bf16[224,1184]{1,0:T(8,128)(2,1)} %get-tuple-element.134), channel_id=1, source_target_pairs={{0,1},{1,0},{2,3},{3,2},{4,5},{5,4},{6,7},{7,6},{8,9},{9,8},{10,11... | collective-permute-start | bytes 1591304 | tf_op jit(solution)/shard_map/ppermute | solution.py:42
  212.6 0.8 copy-start.25
  216.5 0.8 copy-start.26
  (2 other events, 1.4 us)
